TPU v7x, 256 devices: a whole 4x4x8 slice. The times are simulated.
256 devices in a mesh: ctx: 32 (over x, z), head: 8 (over y, core).
Axes of the slice: x: 4, y: 4, z: 8, core: 2. Of those that a mesh axis runs over, the one named last changes fastest.
Arguments:
- query: bfloat16 [16384, 32, 128], P('ctx', 'head'), may hold values from -24 to 24
- key: bfloat16 [16384, 32, 128], P('ctx', 'head'), may hold values from -6 to 6
- value: bfloat16 [16384, 32, 128], P('ctx', 'head'), may hold values from -6 to 6
- out_grad: bfloat16 [16384, 32, 128], P('ctx', 'head'), may hold values from -6 to 6
- random_links: int32 [256, 32, 3], P(None, 'head'), may hold values from 0 to 255, as said below
Outputs:
- attended: bfloat16 [16384, 32, 128], P('ctx', 'head')
- query_grad: bfloat16 [16384, 32, 128], P('ctx', 'head')
- key_grad: bfloat16 [16384, 32, 128], P('ctx', 'head')
- value_grad: bfloat16 [16384, 32, 128], P('ctx', 'head')
Inputs may be any that keep to these rules, and one draw needn't show every extreme that they name: `random_links`: within one head, the 24 random entries of the query blocks o * 8 to o * 8 + 7 name blocks of any one run p * 8 to p * 8 + 7 at most 2 times, and for each such run of query blocks and head some run p is named exactly 2 times.
All inputs are finite; a program needn't handle non-finite values.
Results may differ from a plain program's by a relative error of at most 0.012.
Values may be sent and summed in bfloat16 or wider, within the bound.
A program may use at most 128 MiB of HBM per device.

v0:
```python
import math

import jax
import jax.numpy as jnp
from jax import lax
from jax.sharding import PartitionSpec as P

BLOCK = 64


def extended(cells, sides, width):
    for axis, dim in sides:
        count = lax.axis_size(axis)
        ends = count - 1
        head = lax.slice_in_dim(cells, 0, width, axis=dim)
        tail = lax.slice_in_dim(cells, cells.shape[dim] - width, cells.shape[dim], axis=dim)
        cells = jnp.concatenate(
            [
                lax.ppermute(tail, axis, [(i, (i + 1) % count) for i in range(ends)]),
                cells,
                lax.ppermute(head, axis, [((i + 1) % count, i) for i in range(ends)]),
            ],
            axis=dim,
        )
    return cells


def local(query, key, value, out_grad, random_links):
    seq_local, head_count, head_width = query.shape
    per_device = seq_local // BLOCK
    ctx_size = lax.axis_size("ctx")
    position = lax.axis_index("ctx")
    link_count = random_links.shape[2]
    ref_count = per_device * link_count
    capacity = max(2, (5 * ref_count + 4 * ctx_size - 1) // (4 * ctx_size))
    slot_count = ctx_size * capacity
    block_width = BLOCK * head_width
    scaling = 1.0 / math.sqrt(head_width)
    kind_count = 5 + link_count
    key_length = kind_count * BLOCK

    def head_major(array):
        return array.reshape(per_device, BLOCK, head_count, head_width).transpose(2, 0, 1, 3)

    def seq_major(array):
        return array.transpose(1, 2, 0, 3).reshape(seq_local, head_count, head_width)

    query_heads = head_major(query)
    grad_heads = head_major(out_grad)
    paired = jnp.stack((key, value))
    kv_table = (
        paired.reshape(2, per_device, BLOCK, head_count, head_width)
        .transpose(3, 0, 1, 2, 4)
        .reshape(head_count, 2, per_device, block_width)
    )
    own_links = lax.dynamic_slice_in_dim(random_links, position * per_device, per_device, 0)
    flat_links = own_links.transpose(1, 0, 2).reshape(head_count, ref_count)
    owners = flat_links // per_device
    matches = (owners[:, :, None] == jnp.arange(ctx_size, dtype=jnp.int32)[None, None, :]).astype(
        jnp.int32
    )
    earlier = jnp.cumsum(matches, axis=1) - matches
    placing = owners * capacity + jnp.sum(earlier * matches, axis=2)
    all_links = (
        random_links.reshape(ctx_size, per_device, head_count, link_count)
        .transpose(2, 0, 1, 3)
        .reshape(head_count, ctx_size, ref_count)
    )
    aimed = (all_links // per_device == position).astype(jnp.int32)
    order_inside = jnp.cumsum(aimed, axis=2) - aimed
    picked = aimed[..., None] * (
        order_inside[..., None] == jnp.arange(capacity, dtype=jnp.int32)
    ).astype(jnp.int32)
    wanted = jnp.sum(picked * (all_links % per_device)[..., None], axis=2).reshape(
        head_count, slot_count
    )
    filled = jnp.sum(picked, axis=2).reshape(head_count, slot_count)

    def serve_blocks():
        chosen = jnp.take_along_axis(kv_table, wanted[:, None, :, None], axis=2)
        chosen = jnp.where(filled[:, None, :, None] > 0, chosen, jnp.zeros_like(chosen))
        return chosen.reshape(head_count, 2, ctx_size, capacity, block_width)

    arrived = lax.all_to_all(
        serve_blocks(), "ctx", split_axis=2, concat_axis=2, tiled=True
    ).reshape(head_count, 2, slot_count, block_width)
    widened = extended(paired, (("ctx", 1),), BLOCK)
    widened_heads = widened.reshape(2, per_device + 2, BLOCK, head_count, head_width).transpose(
        3, 0, 1, 2, 4
    )
    leading = jnp.where(position == 0, paired[:, :BLOCK].astype(jnp.float32), 0.0)
    trailing = jnp.where(
        position == ctx_size - 1, paired[:, seq_local - BLOCK :].astype(jnp.float32), 0.0
    )
    global_kv = lax.psum(jnp.stack((leading, trailing), axis=1).astype(jnp.bfloat16), "ctx")
    anchor_heads = global_kv.transpose(3, 0, 1, 2, 4)
    blocks_here = position * per_device + jnp.arange(per_device, dtype=jnp.int32)
    total_blocks = ctx_size * per_device
    usable = jnp.concatenate(
        (
            (blocks_here > 0)[:, None],
            jnp.ones((per_device, 1), bool),
            (blocks_here < total_blocks - 1)[:, None],
            jnp.ones((per_device, kind_count - 3), bool),
        ),
        axis=1,
    )
    col_valid = jnp.repeat(usable, BLOCK, axis=1)

    def collect_keys(widened_one, anchor_one, arrived_one, placing_one):
        window = jnp.stack((widened_one[:, :-2], widened_one[:, 1:-1], widened_one[:, 2:]), axis=2)
        anchors = jnp.broadcast_to(anchor_one[:, None], (2, per_device, 2, BLOCK, head_width))
        remote = arrived_one[:, placing_one].reshape(2, per_device, link_count, BLOCK, head_width)
        return jnp.concatenate((window, anchors, remote), axis=2).reshape(
            2, per_device, key_length, head_width
        )

    def softmax_rows(query_one, key_sets):
        scores = (
            jnp.einsum("ibd,ikd->ibk", query_one, key_sets[0], preferred_element_type=jnp.float32)
            * scaling
        )
        valid_mask = col_valid[:, None, :]
        scores = jnp.where(valid_mask, scores, -1e30)
        row_max = jnp.max(scores, axis=-1, keepdims=True)
        powers = jnp.where(valid_mask, jnp.exp(scores - row_max), 0.0)
        return powers / jnp.sum(powers, axis=-1, keepdims=True)

    def forward_head(operands):
        query_one, widened_one, anchor_one, arrived_one, placing_one = operands
        key_sets = collect_keys(widened_one, anchor_one, arrived_one, placing_one)
        prob_rows = softmax_rows(query_one, key_sets)
        output_one = jnp.einsum(
            "ibk,ikd->ibd",
            prob_rows.astype(jnp.bfloat16),
            key_sets[1],
            preferred_element_type=jnp.float32,
        ).astype(jnp.bfloat16)
        return (output_one, prob_rows)

    attended_heads, stored_probs = lax.map(
        forward_head, (query_heads, widened_heads, anchor_heads, arrived, placing)
    )
    arrived_back = lax.all_to_all(
        serve_blocks(), "ctx", split_axis=2, concat_axis=2, tiled=True
    ).reshape(head_count, 2, slot_count, block_width)

    def backward_head(operands):
        (
            query_one,
            grad_one,
            output_one,
            probs_one,
            widened_one,
            anchor_one,
            arrived_one,
            placing_one,
        ) = operands
        key_sets = collect_keys(widened_one, anchor_one, arrived_one, placing_one)
        prob_rows = softmax_rows(query_one, key_sets)
        row_delta = jnp.sum(grad_one.astype(jnp.float32) * output_one.astype(jnp.float32), axis=-1)
        grad_probs = jnp.einsum(
            "ibd,ikd->ibk", grad_one, key_sets[1], preferred_element_type=jnp.float32
        )
        grad_scores = (prob_rows * (grad_probs - row_delta[..., None])).astype(jnp.bfloat16)
        query_part = (
            scaling
            * jnp.einsum(
                "ibk,ikd->ibd", grad_scores, key_sets[0], preferred_element_type=jnp.float32
            )
        ).astype(jnp.bfloat16)
        key_part = scaling * jnp.einsum(
            "ibk,ibd->ikd", grad_scores, query_one, preferred_element_type=jnp.float32
        )
        value_part = jnp.einsum(
            "ibk,ibd->ikd",
            prob_rows.astype(jnp.bfloat16),
            grad_one,
            preferred_element_type=jnp.float32,
        )
        pieces = jnp.stack((key_part, value_part)).reshape(
            2, per_device, kind_count, BLOCK, head_width
        )
        nearby = pieces[:, :, 1]
        nearby = nearby.at[:, :-1].add(pieces[:, 1:, 0])
        nearby = nearby.at[:, 1:].add(pieces[:, :-1, 2])
        edge_out = jnp.stack((pieces[:, 0, 0], pieces[:, -1, 2]), axis=1)
        anchor_part = jnp.sum(pieces[:, :, 3:5], axis=1)
        remote = pieces[:, :, 5:].astype(jnp.bfloat16).reshape(2, ref_count, block_width)
        send_back = (
            jnp.zeros((2, slot_count, block_width), jnp.bfloat16).at[:, placing_one].set(remote)
        )
        return (query_part, nearby, edge_out, anchor_part, send_back)

    query_grads, nearby_heads, edge_heads, anchor_grads, send_heads = lax.map(
        backward_head,
        (
            query_heads,
            grad_heads,
            attended_heads,
            stored_probs,
            widened_heads,
            anchor_heads,
            arrived_back,
            placing,
        ),
    )
    edge_in = extended(edge_heads.astype(jnp.bfloat16), (("ctx", 2),), 1).astype(edge_heads.dtype)
    nearby_heads = nearby_heads.at[:, :, 0].add(edge_in[:, :, 0])
    nearby_heads = nearby_heads.at[:, :, -1].add(edge_in[:, :, 3])
    anchor_sums = lax.psum(anchor_grads, "ctx")
    nearby_heads = nearby_heads.at[:, :, 0].add(jnp.where(position == 0, anchor_sums[:, :, 0], 0.0))
    nearby_heads = nearby_heads.at[:, :, -1].add(
        jnp.where(position == ctx_size - 1, anchor_sums[:, :, 1], 0.0)
    )
    returned = lax.all_to_all(
        send_heads.reshape(head_count, 2, ctx_size, capacity, block_width),
        "ctx",
        split_axis=2,
        concat_axis=2,
        tiled=True,
    )
    returned = returned.reshape(head_count, 2, slot_count, block_width)
    landing = (
        (wanted[:, :, None] == jnp.arange(per_device, dtype=jnp.int32)[None, None, :])
        & (filled[:, :, None] > 0)
    ).astype(jnp.bfloat16)
    landed = jnp.einsum("hqj,hxqe->hxje", landing, returned, preferred_element_type=jnp.float32)
    summed = nearby_heads + landed.reshape(head_count, 2, per_device, BLOCK, head_width)
    attended = seq_major(attended_heads)
    query_grad = seq_major(query_grads)
    key_grad = seq_major(summed[:, 0]).astype(jnp.bfloat16)
    value_grad = seq_major(summed[:, 1]).astype(jnp.bfloat16)
    return (attended, query_grad, key_grad, value_grad)


def solution(mesh):
    placed = (
        P("ctx", "head", None),
        P("ctx", "head", None),
        P("ctx", "head", None),
        P("ctx", "head", None),
        P(None, "head", None),
    )
    return jax.shard_map(
        local,
        mesh=mesh,
        in_specs=placed,
        out_specs=(
            P("ctx", "head", None),
            P("ctx", "head", None),
            P("ctx", "head", None),
            P("ctx", "head", None),
        ),
        check_vma=False,
    )
```

profile of v0, /device:TPU:16, one launch (start us, length us, event | category | flops | bytes accessed | tf_op | source)
XLA Modules:
  0.0 753.3 jit_solution(16983627592762365282)
XLA Ops:
  12.1 22.7 %gather_fusion.2 = bf16[256,2,8192]{2,1,0:T(2,128)(2,1)} fusion(bf16[4,2,8,8192]{3,1,2,0:T(2,128)(2,1)S(1)} %copy.253, s32[256]{0:T(256)S(1)} %reshape.658), kind=kCustom, calls=%fused_computation.clone | custom fusion | bytes 16779264 | tf_op jit(solution)/shard_map/jit(take_along_axis)/gather | solution.py:80
  34.7 11.4 %broadcast_select_fusion.1 = bf16[4,2,64,8192]{3,1,2,0:T(2,128)(2,1)S(1)} fusion(pred[4,64]{1,0:T(4,128)(4,1)S(1)} %gt.31, bf16[4,64,2,8192]{3,2,1,0:T(2,128)(2,1)} %bitcast.423, pred[4,64]{1,0:T(4,128)(4,1)S(1)} %and_bitcast_fusion), kind=kLoop, calls=%fused_computation.129 | loop fusion | flops 8388608 | bytes 16777728 | tf_op jit(solution)/shard_map/jit(_where)/select_n | solution.py:81
  46.1 7.5 copy.254
  53.6 11.5 %all-to-all-start = ((bf16[4,2,32,2,8192]{4,1,3,0,2:T(2,128)(2,1)}), bf16[4,2,32,2,8192]{4,1,3,0,2:T(2,128)(2,1)}, u32[]{:S(2)}, u32[]{:S(2)}) async-start(bf16[4,2,32,2,8192]{4,1,3,0,2:T(2,128)(2,1)} %copy.254), calls=%async_computation | async-start | bytes 16777216 | tf_op jit(solution)/shard_map/all_to_all | solution.py:84
  66.2 3.6 collective-permute-start
  73.2 184.9 %collective-permute-done = bf16[2,64,4,128]{3,1,0,2:T(8,128)(2,1)S(1)} collective-permute-done((bf16[2,64,4,128]{3,1,0,2:T(8,128)(2,1)S(1)}, bf16[2,64,4,128]{3,1,0,2:T(8,128)(2,1)S(1)}, u32[]{:S(2)}, u32[]{:S(2)}) %collective-permute-start) | collective-permute-done | bytes 131104 | tf_op jit(solution)/shard_map/ppermute | solution.py:19
  259.3 8.6 %copy.255 = bf16[4,2,32,2,8192]{4,1,3,2,0:T(2,128)(2,1)} copy(bf16[4,2,32,2,8192]{4,1,3,0,2:T(2,128)(2,1)} %all-to-all-done) | data formatting | bytes 16777216 | tf_op jit(solution)/shard_map/all_to_all | solution.py:84
  267.8 19.2 %all-reduce.3.cloned.1.call-done = bf16[4,2,2,64,128]{4,3,2,1,0:T(8,128)(2,1)} async-done(((bf16[4,2,2,64,128]{4,3,2,1,0:T(8,128)(2,1)}), bf16[4,2,2,64,128]{4,3,2,1,0:T(8,128)(2,1)}) %all-reduce.3.cloned.1.call-update) | async-done | bytes 262160 | tf_op jit(solution)/shard_map/psum | solution.py:95
  288.0 67.3 %while.40 = (s32[]{:T(128)}, bf16[4,8,64,128]{3,2,1,0:T(8,128)(2,1)}, bf16[4,8,64,128]{3,2,1,0:T(8,128)(2,1)S(1)}, bf16[4,2,10,64,128]{4,3,2,1,0:T(8,128)(2,1)},...) while((s32[]{:T(128)}, ...), condition=%wide.region_9.11_spmd.clone.clone, body=%wide.region_6.10_spmd.clone.sunk.clone | while | flops 136645184 | bytes 22645300 | solution.py:141
  293.4 3.4 dynamic-slice_bitcast_fusion.21
  296.8 2.1 gather_fusion
  310.2 3.4 dynamic-slice_bitcast_fusion.21
  313.6 2.1 gather_fusion
  327.0 3.4 dynamic-slice_bitcast_fusion.21
  330.4 2.1 gather_fusion
  343.8 3.4 dynamic-slice_bitcast_fusion.21
  347.2 2.1 gather_fusion
  356.2 140.3 %while.41 = (s32[]{:T(128)}, bf16[4,8,64,128]{3,2,1,0:T(8,128)(2,1)}, f32[4,2,8,64,128]{4,3,1,2,0:T(8,128)}, bf16[4,2,2,64,128]{4,3,1,2,0:T(8,128)(2,1)}, f32[4,...) while((s32[]{:T(128)}, ...), condition=%wide.region_16.18_spmd.clone.clone, body=%wide.region_10.17_spmd.clone.sunk.clone | while | flops 341624896 | bytes 79274800 | solution.py:195
  362.9 3.4 dynamic-slice_bitcast_fusion.24
  366.3 2.1 gather_fusion.1
  377.9 2.3 fusion.240
  384.5 2.0 broadcast.552
  388.1 3.2 bitcast_dynamic-update-slice_fusion.7
  398.0 3.4 dynamic-slice_bitcast_fusion.24
  401.4 2.1 gather_fusion.1
  413.0 2.3 fusion.240
  419.7 2.0 broadcast.552
  423.3 3.1 bitcast_dynamic-update-slice_fusion.7
  433.1 3.4 dynamic-slice_bitcast_fusion.24
  436.5 2.1 gather_fusion.1
  448.1 2.3 fusion.240
  454.7 2.0 broadcast.552
  458.3 3.2 bitcast_dynamic-update-slice_fusion.7
  468.2 3.4 dynamic-slice_bitcast_fusion.24
  471.6 2.1 gather_fusion.1
  483.2 2.3 fusion.240
  489.8 2.0 broadcast.552
  493.4 3.2 bitcast_dynamic-update-slice_fusion.7
  496.5 16.4 %copy.260 = bf16[4,2,32,2,8192]{4,3,1,0,2:T(2,128)(2,1)} copy(bf16[4,2,32,2,8192]{4,1,3,2,0:T(2,128)(2,1)} %bitcast.428) | data formatting | bytes 16777216 | tf_op jit(solution)/shard_map/reshape | solution.py:217
  512.9 5.8 all-to-all-start.1
  518.9 3.8 collective-permute-start.2
  525.3 2.2 copy.259
  527.5 175.7 %collective-permute-done.2 = bf16[4,2,1,64,128]{4,3,1,2,0:T(8,128)(2,1)S(1)} collective-permute-done((bf16[4,2,1,64,128]{4,3,1,2,0:T(8,128)(2,1)S(1)}, bf16[4,2,1,64,128]{4,3,1,2,0:T(8,128)(2,1)S(1)}, u32[]{:S(2)}, u32[]{:S(2)}) %collective-permute-start.2) | collective-permute-done | bytes 131104 | tf_op jit(solution)/shard_map/ppermute | solution.py:19
  703.2 3.0 collective-permute-done.3
  706.3 8.8 %all-reduce.5.cloned.1.call-done = f32[4,2,2,64,128]{4,3,1,2,0:T(8,128)} async-done(((f32[4,2,2,64,128]{4,3,1,2,0:T(8,128)}), f32[4,2,2,64,128]{4,3,1,2,0:T(8,128)}) %all-reduce.5.cloned.1.call-update) | async-done | bytes 524304 | tf_op jit(solution)/shard_map/psum | solution.py:211
  717.2 8.5 %copy.261 = bf16[4,2,32,2,8192]{4,3,2,1,0:T(2,128)(2,1)} copy(bf16[4,2,32,2,8192]{4,3,1,0,2:T(2,128)(2,1)} %all-to-all-done.1) | data formatting | bytes 16777216 | tf_op jit(solution)/shard_map/all_to_all | solution.py:216
  725.8 13.1 %reshape.606 = bf16[4,2,64,8192]{3,2,1,0:T(8,128)(2,1)} reshape(bf16[4,2,32,2,8192]{4,3,2,1,0:T(2,128)(2,1)} %copy.261) | data formatting | bytes 16777216 | tf_op jit(solution)/shard_map/reshape | solution.py:223
  738.8 4.6 convolution_bitcast_fusion
  (305 shorter events, 152.8 us)
Async XLA Ops:
  7.2 2.9 copy-start.6
  7.2 3.1 copy-start.7
  9.6 0.6 copy-start.10
  10.0 24.7 %copy-start.13 = (pred[4,64]{1,0:T(4,128)(4,1)}, pred[4,64]{1,0:T(4,128)(4,1)S(1)}, u32[]{:S(2)}) copy-start(pred[4,64]{1,0:T(4,128)(4,1)S(1)} %gt.31) | copy-start | bytes 772
  53.6 205.7 %all-to-all-start = ((bf16[4,2,32,2,8192]{4,1,3,0,2:T(2,128)(2,1)}), bf16[4,2,32,2,8192]{4,1,3,0,2:T(2,128)(2,1)}, u32[]{:S(2)}, u32[]{:S(2)}) async-start(bf16[4,2,32,2,8192]{4,1,3,0,2:T(2,128)(2,1)} %copy.254), calls=%async_computation | async-start | bytes 16777216 | tf_op jit(solution)/shard_map/all_to_all | solution.py:84
  65.1 222.0 %all-reduce.3.cloned.1.call-start = ((), (), s32[]{:S(2)}) async-start(), calls=%async_computation.2 | async-start | bytes 524288 | tf_op jit(solution)/shard_map/psum | solution.py:95
  65.2 6.4 copy-start.12
  65.2 6.8 copy-start.8
  65.3 6.7 copy-start.9
  66.2 191.9 %collective-permute-start = (bf16[2,64,4,128]{3,1,0,2:T(8,128)(2,1)S(1)}, bf16[2,64,4,128]{3,1,0,2:T(8,128)(2,1)S(1)}, u32[]{:S(2)}, u32[]{:S(2)}) collective-permute-start(bf16[2,64,4,128]{3,1,0,2:T(8,128)(2,1)S(1)} %get-tuple-element.445), channel_id=1, source_target_pairs={{0,8},{8,16},{16,24},{24,32},{32,40},{40,48},{48,56},{56,64},{64,7... | collective-permute-start | bytes 393224 | tf_op jit(solution)/shard_map/ppermute | solution.py:19
  69.8 188.3 %collective-permute-start.1 = (bf16[2,64,4,128]{3,1,0,2:T(8,128)(2,1)S(1)}, bf16[2,64,4,128]{3,1,0,2:T(8,128)(2,1)S(1)}, u32[]{:S(2)}, u32[]{:S(2)}) collective-permute-start(bf16[2,64,4,128]{3,1,0,2:T(8,128)(2,1)S(1)} %get-tuple-element.457), channel_id=1, source_target_pairs={{8,0},{16,8},{24,16},{32,24},{40,32},{48,40},{56,48},{64,56},{72,6... | collective-permute-start | bytes 393224 | tf_op jit(solution)/shard_map/ppermute | solution.py:21
  356.2 10.1 %copy-start.1 = (bf16[4,8,64,128]{3,2,1,0:T(8,128)(2,1)}, bf16[4,8,64,128]{3,2,1,0:T(8,128)(2,1)S(1)}, u32[]{:S(2)}) copy-start(bf16[4,8,64,128]{3,2,1,0:T(8,128)(2,1)S(1)} %get-tuple-element.729) | copy-start | bytes 1572868 | tf_op jit(solution)/shard_map/while
  376.1 0.8 copy-start
  388.1 3.2 copy-start.2
  391.4 10.1 %copy-start.1 = (bf16[4,8,64,128]{3,2,1,0:T(8,128)(2,1)}, bf16[4,8,64,128]{3,2,1,0:T(8,128)(2,1)S(1)}, u32[]{:S(2)}) copy-start(bf16[4,8,64,128]{3,2,1,0:T(8,128)(2,1)S(1)} %get-tuple-element.729) | copy-start | bytes 1572868 | tf_op jit(solution)/shard_map/while
  411.3 0.8 copy-start
  423.3 3.1 copy-start.2
  426.4 10.1 %copy-start.1 = (bf16[4,8,64,128]{3,2,1,0:T(8,128)(2,1)}, bf16[4,8,64,128]{3,2,1,0:T(8,128)(2,1)S(1)}, u32[]{:S(2)}) copy-start(bf16[4,8,64,128]{3,2,1,0:T(8,128)(2,1)S(1)} %get-tuple-element.729) | copy-start | bytes 1572868 | tf_op jit(solution)/shard_map/while
  446.3 0.8 copy-start
  458.3 3.2 copy-start.2
  461.5 10.1 %copy-start.1 = (bf16[4,8,64,128]{3,2,1,0:T(8,128)(2,1)}, bf16[4,8,64,128]{3,2,1,0:T(8,128)(2,1)S(1)}, u32[]{:S(2)}) copy-start(bf16[4,8,64,128]{3,2,1,0:T(8,128)(2,1)S(1)} %get-tuple-element.729) | copy-start | bytes 1572868 | tf_op jit(solution)/shard_map/while
  481.4 0.8 copy-start
  493.3 3.2 copy-start.2
  512.9 5.9 copy-start.5
  512.9 11.0 %copy-start.11 = (s32[4,32,2]{0,2,1:T(2,128)S(1)}, s32[4,32,2]{0,2,1:T(2,128)}, u32[]{:S(2)}) copy-start(s32[4,32,2]{0,2,1:T(2,128)} %copy-done.10) | copy-start | bytes 3076
  512.9 11.1 %copy-start.3 = (bf16[4,8,64,128]{3,2,1,0:T(8,128)(2,1)S(1)}, bf16[4,8,64,128]{3,2,1,0:T(8,128)(2,1)}, u32[]{:S(2)}) copy-start(bf16[4,8,64,128]{3,2,1,0:T(8,128)(2,1)} %get-tuple-element.745) | copy-start | bytes 1572868
  512.9 204.3 %all-to-all-start.1 = ((bf16[4,2,32,2,8192]{4,3,1,0,2:T(2,128)(2,1)}), bf16[4,2,32,2,8192]{4,3,1,0,2:T(2,128)(2,1)}, u32[]{:S(2)}, u32[]{:S(2)}) async-start(bf16[4,2,32,2,8192]{4,3,1,0,2:T(2,128)(2,1)} %copy.260), calls=%async_computation.1 | async-start | bytes 16777216 | tf_op jit(solution)/shard_map/all_to_all | solution.py:216
  518.8 187.4 %copy-start.4 = (f32[4,2,8,64,128]{4,3,1,2,0:T(8,128)S(1)}, f32[4,2,8,64,128]{4,3,1,2,0:T(8,128)}, u32[]{:S(2)}) copy-start(f32[4,2,8,64,128]{4,3,1,2,0:T(8,128)} %get-tuple-element.300) | copy-start | bytes 6291460
  518.8 196.4 %all-reduce.5.cloned.1.call-start = ((), (), s32[]{:S(2)}) async-start(), calls=%async_computation.3 | async-start | bytes 1048576 | tf_op jit(solution)/shard_map/psum | solution.py:211
  518.9 184.3 %collective-permute-start.2 = (bf16[4,2,1,64,128]{4,3,1,2,0:T(8,128)(2,1)S(1)}, bf16[4,2,1,64,128]{4,3,1,2,0:T(8,128)(2,1)S(1)}, u32[]{:S(2)}, u32[]{:S(2)}) collective-permute-start(bf16[4,2,1,64,128]{4,3,1,2,0:T(8,128)(2,1)S(1)} %get-tuple-element.458), channel_id=1, source_target_pairs={{0,8},{8,16},{16,24},{24,32},{32,40},{40,48},{48,56},{56,64},{64,7... | collective-permute-start | bytes 393224 | tf_op jit(solution)/shard_map/ppermute | solution.py:19
  522.6 183.6 %collective-permute-start.3 = (bf16[4,2,1,64,128]{4,3,1,2,0:T(8,128)(2,1)S(1)}, bf16[4,2,1,64,128]{4,3,1,2,0:T(8,128)(2,1)S(1)}, u32[]{:S(2)}, u32[]{:S(2)}) collective-permute-start(bf16[4,2,1,64,128]{4,3,1,2,0:T(8,128)(2,1)S(1)} %get-tuple-element.459), channel_id=1, source_target_pairs={{8,0},{16,8},{24,16},{32,24},{40,32},{48,40},{56,48},{64,56},{72,6... | collective-permute-start | bytes 393224 | tf_op jit(solution)/shard_map/ppermute | solution.py:21
  725.7 13.1 %copy-start.14 = (pred[4,64]{1,0:T(4,128)(4,1)S(1)}, pred[4,64]{1,0:T(4,128)(4,1)}, u32[]{:S(2)}) copy-start(pred[4,64]{1,0:T(4,128)(4,1)} %copy-done.13) | copy-start | bytes 772
Sparse Core Ops, SparseCore 0:
  70.0 217.0 all-reduce.2
  524.1 191.0 all-reduce.4
where the time goes:
time: 756 us; the launch traced here: 753 us
  waiting for transfers between devices  392 us (52%)
  local copies, waits for them, and re-layouts  241 us (32%)
  matrix products  43.7 us (6%)
  other arithmetic  34 us (4%)
  starting transfers between devices  27.5 us (4%)
  between operations  14.5 us (2%)
    ppermute x2, waiting for transfers between devices, extended(): lax.ppermute(tail, axis, [(i, (i + 1) % count) for i in range(ends)])  361 us
    squeeze x16, local copies, waits for them, and re-layouts, local(): lax.map(forward_head, (query_heads, widened_heads, anchor_heads, arrived,...  35 us
    while x60, local copies, waits for them, and re-layouts  30.1 us
    gather x2, local copies, waits for them, and re-layouts, serve_blocks(): chosen = jnp.take_along_axis(kv_table, wanted[:, None, :, None], axis=2)  22.7 us
    psum x1, waiting for transfers between devices, local(): lax.psum(jnp.stack((leading, trailing), axis=1).astype(jnp.bfloat16), 'ctx')  19.2 us
    dynamic_update_slice x12, local copies, waits for them, and re-layouts, local(): lax.map(backward_head, (query_heads, grad_heads, attended_heads, stored_p...  18.8 us
    gather x8, local copies, waits for them, and re-layouts, collect_keys(): arrived_one[:, placing_one]  17 us
    reshape x1, local copies, waits for them, and re-layouts, local(): send_heads.reshape(head_count, 2, ctx_size, capacity, block_width)  16.4 us
  transfers between devices with their start and end apart: 8, of which 5 were waited for; matrix products, arithmetic and copies ran while one was open for 2% of the time, Pallas kernels for 0%

commit v1 on v0

v1 whole, which is shorter than its diff:
```python
import math

import jax
import jax.numpy as jnp
from jax import lax
from jax.experimental import pallas as pl
from jax.experimental.pallas import tpu as pltpu
from jax.sharding import PartitionSpec as P

BLOCK = 64
HD = 128
NX = 4
NZ = 8
BPD = 8
HALF = BPD // 2
H = 4
R = 3
REFS = BPD * R
TARGETS = NZ * BPD
MAIN = 16
RELAY = 8
MERGED = MAIN + 2
RELAYED = RELAY + 1
FROM_R, FROM_L, OWN = 0, MERGED, 2 * MERGED
RECEIVED = OWN + MAIN
B_RR = 2 * MERGED
B_RL = B_RR + RELAY
B_OWN = B_RL + RELAY
B_ZERO = B_OWN + MAIN
B_SIZE = B_ZERO + 1
DEEP = 8
F32 = jnp.float32
BF16 = jnp.bfloat16
MESH = pl.DeviceIdType.MESH
SCALE = 1.0 / math.sqrt(HD)


def slot_tables(links):
    ctx = lax.axis_index("ctx")
    x, z = ctx // NZ, ctx % NZ
    row = lax.dynamic_slice_in_dim(links.reshape(NX, NZ, BPD, H, R), z, 1, 1)[:, 0]
    named = row.transpose(2, 0, 1, 3).reshape(H, NX, REFS)
    planes = jnp.arange(NX, dtype=jnp.int32)
    away = (named // TARGETS - planes[None, :, None]) % NX
    target = named % TARGETS
    entry = jnp.arange(REFS, dtype=jnp.int32)
    before = entry[None, :] < entry[:, None]
    rank = jnp.sum(
        ((away[..., None, :] == away[..., :, None]) & before).astype(jnp.int32), axis=-1
    )
    n_r = jnp.sum((away == 1).astype(jnp.int32), axis=-1)
    n_o = jnp.sum((away == 2).astype(jnp.int32), axis=-1)
    n_l = jnp.sum((away == 3).astype(jnp.int32), axis=-1)
    by_right = jnp.minimum(n_o, jnp.minimum(RELAY, MAIN - n_r))[..., None]
    right_way = rank < by_right
    place = jnp.where(
        away == 0,
        OWN + rank,
        jnp.where(
            away == 1,
            FROM_R + rank,
            jnp.where(
                away == 3,
                FROM_L + rank,
                jnp.where(
                    right_way,
                    FROM_R + n_r[..., None] + rank,
                    FROM_L + n_l[..., None] + rank - by_right,
                ),
            ),
        ),
    )
    relay_rank = jnp.where(right_way, rank, rank - by_right)
    code = jnp.where(away == 2, TARGETS + relay_rank, target)
    spots = jnp.arange(RECEIVED, dtype=jnp.int32)
    hit = place[..., None] == spots
    merged = jnp.sum(jnp.where(hit, code[..., None], 0), axis=2)
    relay_place = jnp.where(away == 2, jnp.where(right_way, 0, RELAY) + relay_rank, -1)
    relays = jnp.sum(
        jnp.where(
            relay_place[..., None] == jnp.arange(2 * RELAY, dtype=jnp.int32), target[..., None], 0
        ),
        axis=2,
    )
    own_place = lax.dynamic_slice_in_dim(place, x, 1, 1)[:, 0]
    giver = jnp.sum(
        jnp.where(own_place[..., None] == spots, entry[None, :, None], 0), axis=1
    )
    landing = jnp.where(
        away == 0,
        B_OWN + rank,
        jnp.where(
            away == 1,
            FROM_L + rank,
            jnp.where(
                away == 3, FROM_R + rank, jnp.where(right_way, B_RL, B_RR) + relay_rank
            ),
        ),
    ).reshape(H, NX * REFS)
    here = jnp.where(named // TARGETS == x, target, -1).reshape(H, NX * REFS)
    every = jnp.arange(NX * REFS, dtype=jnp.int32)
    same = (here[:, None, :] == here[:, :, None]) & (every[None, :] < every[:, None])
    depth = jnp.sum(same.astype(jnp.int32), axis=-1)
    cell = jnp.where(here >= 0, here * DEEP + depth, -1)
    cells = jnp.arange(TARGETS * DEEP, dtype=jnp.int32)
    sources = B_ZERO + jnp.sum(
        jnp.where(cell[:, :, None] == cells, landing[:, :, None] - B_ZERO, 0), axis=1
    )
    counts = jnp.stack((n_r, n_l), axis=-1).reshape(H, 2 * NX)
    return (
        merged.reshape(H, NX * RECEIVED),
        relays.reshape(H, NX * 2 * RELAY),
        own_place,
        giver,
        counts,
        sources,
    )


def kernel(
    kv,
    query,
    grad,
    merged_t,
    relay_t,
    place_t,
    giver_t,
    count_t,
    source_t,
    out_o,
    out_q,
    out_k,
    out_v,
    table,
    relay_out,
    relay_in,
    merged_out,
    received,
    terms_in,
    terms_relay,
    sums_r,
    sums_l,
    near,
    anchor_acc,
    anchor_kv,
    wide,
    terms,
    ag_send,
    ag_recv,
    f1_send,
    f1_recv,
    f2_send,
    f2_recv,
    b1_send,
    b1_recv,
    b2_send,
    b2_recv,
    rs_send,
    rs_recv,
):
    ctx = lax.axis_index("ctx")
    x, z = ctx // NZ, ctx % NZ
    z_r = x * NZ + lax.rem(z + 1, NZ)
    z_l = x * NZ + lax.rem(z + NZ - 1, NZ)
    p_r = lax.rem(x + 1, NX)
    p_l = lax.rem(x + NX - 1, NX)
    p_o = lax.rem(x + 2, NX)
    x_r = p_r * NZ + z
    x_l = p_l * NZ + z

    def to(device, src, dst, send, recv):
        return pltpu.make_async_remote_copy(
            src_ref=src,
            dst_ref=dst,
            send_sem=send,
            recv_sem=recv,
            device_id={"ctx": device},
            device_id_type=MESH,
        )

    barrier = pltpu.get_barrier_semaphore()
    for device in (z_r, z_l, x_r, x_l):
        pl.semaphore_signal(barrier, inc=1, device_id={"ctx": device}, device_id_type=MESH)
    pl.semaphore_wait(barrier, 4)

    def gather_copy(h, s, half, right):
        row = lax.rem(z + NZ - (s - 1), NZ) if right else lax.rem(z + s - 1, NZ)
        src = (
            kv.at[h, pl.ds(half * HALF, HALF)]
            if s == 1
            else table[h].at[pl.ds(row * BPD + half * HALF, HALF)]
        )
        dst = table[h].at[pl.ds(row * BPD + half * HALF, HALF)]
        way = 0 if right else 1
        return to(
            z_r if right else z_l, src, dst, ag_send.at[h, s - 1, half, way],
            ag_recv.at[h, s - 1, half, way],
        )

    def gather_moves(s):
        return [
            (half, right)
            for half in (0, 1)
            for right in (True, False)
            if s < 4 or right == (half == 0)
        ]

    def gather_start(h):
        for half, right in gather_moves(1):
            gather_copy(h, 1, half, right).start()

    def gather_step(h, s):
        for half, right in gather_moves(s - 1):
            gather_copy(h, s - 1, half, right).wait_recv()
            if (half, right) in gather_moves(s):
                gather_copy(h, s, half, right).start()

    def gather_end(h):
        for half, right in gather_moves(4):
            gather_copy(h, 4, half, right).wait_recv()

    def gather_sent(h):
        for s in (1, 2, 3, 4):
            for half, right in gather_moves(s):
                gather_copy(h, s, half, right).wait_send()

    def place_own(h):
        @pl.loop(0, BPD)
        def _(b):
            table[h][z * BPD + b] = kv[h, b]

    def relay_copy(h, side):
        return to(
            (x_r, x_l)[side], relay_out[h].at[side], relay_in[h].at[1 - side],
            f1_send.at[h, side], f1_recv.at[h, side],
        )

    def merged_copy(h, side):
        return to(
            (x_r, x_l)[side],
            merged_out[h].at[side],
            received[h].at[pl.ds((FROM_L, FROM_R)[side], MERGED)],
            f2_send.at[h, side],
            f2_recv.at[h, side],
        )

    def send_relays(h):
        @pl.loop(0, RELAY)
        def _(k):
            relay_out[h][0, k] = table[h][relay_t[h, p_o * 2 * RELAY + RELAY + k]]
            relay_out[h][1, k] = table[h][relay_t[h, p_o * 2 * RELAY + k]]

        corner = jnp.where(x == 0, table[h][0], table[h][TARGETS - 1])
        relay_out[h][0, RELAY] = corner
        relay_out[h][1, RELAY] = corner
        for side in (0, 1):
            relay_copy(h, side).start()

        @pl.loop(0, MAIN)
        def _(k):
            received[h][OWN + k] = table[h][merged_t[h, x * RECEIVED + OWN + k]]

    def send_merged(h):
        for side in (0, 1):
            relay_copy(h, side).wait_recv()

        @pl.loop(0, MAIN)
        def _(k):
            for side, plane, first, back in ((0, p_r, FROM_L, 1), (1, p_l, FROM_R, 0)):
                code = merged_t[h, plane * RECEIVED + first + k]
                direct = table[h][jnp.minimum(code, TARGETS - 1)]
                passed = relay_in[h][back, jnp.maximum(code - TARGETS, 0)]
                merged_out[h][side, k] = jnp.where(code < TARGETS, direct, passed)

        merged_out[h][0, MAIN] = relay_in[h][1, RELAY]
        merged_out[h][1, MAIN] = relay_in[h][0, RELAY]
        merged_out[h][0, MAIN + 1] = table[h][TARGETS - 1]
        merged_out[h][1, MAIN + 1] = table[h][0]
        for side in (0, 1):
            merged_copy(h, side).start()

    def compute(h):
        for side in (0, 1):
            merged_copy(h, side).wait_recv()
        above = jnp.where(
            z > 0,
            table[h][lax.rem(z + NZ - 1, NZ) * BPD + BPD - 1],
            received[h][FROM_L + MAIN + 1],
        )
        below = jnp.where(z < NZ - 1, table[h][lax.rem(z + 1, NZ) * BPD], received[h][FROM_R + MAIN + 1])
        relay_r, relay_l = relay_in[h][0, RELAY], relay_in[h][1, RELAY]
        first = jnp.where(
            x == 0,
            table[h][0],
            jnp.where(x == 1, relay_l, jnp.where(x == 3, relay_r, received[h][FROM_L + MAIN])),
        )
        last = jnp.where(
            x == 3,
            table[h][TARGETS - 1],
            jnp.where(x == 2, relay_r, jnp.where(x == 0, relay_l, received[h][FROM_R + MAIN])),
        )
        for p in (0, 1):
            wide[p, 0:BLOCK] = above[p]
            wide[p, BLOCK * (BPD + 1) : BLOCK * (BPD + 2)] = below[p]
            anchor_kv[p, 0:BLOCK] = first[p]
            anchor_kv[p, BLOCK : 2 * BLOCK] = last[p]
            for b in range(BPD):
                wide[p, BLOCK * (b + 1) : BLOCK * (b + 2)] = kv[h, b, p]
        near[h][...] = jnp.zeros_like(near[h])
        anchor_acc[h][...] = jnp.zeros_like(anchor_acc[h])
        column = lax.broadcasted_iota(jnp.int32, (1, 8 * BLOCK), 1)

        @pl.loop(0, BPD)
        def _(i):
            rows = pl.ds(pl.multiple_of(i * BLOCK, BLOCK), 3 * BLOCK)
            spots = [place_t[h, i * R + r] for r in range(R)]
            keys, values = (
                jnp.concatenate(
                    [wide[p, rows], anchor_kv[p]] + [received[h][s, p] for s in spots], axis=0
                )
                for p in (0, 1)
            )
            q, g = query[h, i], grad[h, i]
            block = ctx * BPD + i
            low = jnp.where(block == 0, BLOCK, 0)
            cut = jnp.where(block == NX * NZ * BPD - 1, 2 * BLOCK, 3 * BLOCK)
            masked = (column < low) | ((column >= cut) & (column < 3 * BLOCK))
            contract_last = (((1,), (1,)), ((), ()))
            contract_first = (((0,), (0,)), ((), ()))
            scores = lax.dot_general(q, keys, contract_last, preferred_element_type=F32) * SCALE
            scores = jnp.where(masked, -1e30, scores)
            powers = jnp.exp(scores - jnp.max(scores, axis=-1, keepdims=True))
            probs = powers * (1.0 / jnp.sum(powers, axis=-1, keepdims=True))
            low_probs = probs.astype(BF16)
            attended = jnp.dot(low_probs, values, preferred_element_type=F32).astype(BF16)
            out_o[h, i] = attended
            delta = jnp.sum(g.astype(F32) * attended.astype(F32), axis=-1, keepdims=True)
            grad_probs = lax.dot_general(g, values, contract_last, preferred_element_type=F32)
            grad_scores = (probs * (grad_probs - delta)).astype(BF16)
            out_q[h, i] = (
                jnp.dot(grad_scores, keys, preferred_element_type=F32) * SCALE
            ).astype(BF16)
            key_part = (
                lax.dot_general(grad_scores, q, contract_first, preferred_element_type=F32) * SCALE
            )
            value_part = lax.dot_general(
                low_probs, g, contract_first, preferred_element_type=F32
            )
            for p, part in ((0, key_part), (1, value_part)):
                near[h][p, rows] += part[: 3 * BLOCK]
                anchor_acc[h][p] += part[3 * BLOCK : 5 * BLOCK]
                for r in range(R):
                    terms[i * R + r, p] = part[(5 + r) * BLOCK : (6 + r) * BLOCK].astype(BF16)

    def terms_copy(h, side):
        return to(
            (x_r, x_l)[side],
            merged_out[h].at[side],
            terms_in[h].at[pl.ds((FROM_L, FROM_R)[side], MERGED)],
            b1_send.at[h, side],
            b1_recv.at[h, side],
        )

    def terms_relay_copy(h, side):
        return to(
            (x_r, x_l)[side], relay_out[h].at[side], terms_relay[h].at[1 - side],
            b2_send.at[h, side], b2_recv.at[h, side],
        )

    def anchor(h, which):
        return anchor_acc[h][:, which * BLOCK : (which + 1) * BLOCK]

    def send_terms(h):
        for side in (0, 1):
            merged_copy(h, side).wait_send()

        @pl.loop(0, MAIN)
        def _(k):
            merged_out[h][0, k] = terms[giver_t[h, FROM_R + k]]
            merged_out[h][1, k] = terms[giver_t[h, FROM_L + k]]
            terms_in[h][B_OWN + k] = terms[giver_t[h, OWN + k]]

        terms_in[h][B_ZERO] = jnp.zeros((2, BLOCK, HD), BF16)
        merged_out[h][0, MAIN] = anchor(h, 1).astype(BF16)
        merged_out[h][1, MAIN] = anchor(h, 0).astype(BF16)
        merged_out[h][0, MAIN + 1] = near[h][:, (BPD + 1) * BLOCK :].astype(BF16)
        merged_out[h][1, MAIN + 1] = near[h][:, :BLOCK].astype(BF16)
        for side in (0, 1):
            terms_copy(h, side).start()

    def relay_terms(h):
        for side in (0, 1):
            relay_copy(h, side).wait_send()
            terms_copy(h, side).wait_recv()

        @pl.loop(0, RELAY)
        def _(k):
            from_left = count_t[h, p_l * 2] + k
            from_right = count_t[h, p_r * 2 + 1] + k
            relay_out[h][0, k] = terms_in[h][FROM_L + jnp.minimum(from_left, MAIN - 1)]
            relay_out[h][1, k] = terms_in[h][FROM_R + jnp.minimum(from_right, MAIN - 1)]

        first, last = anchor(h, 0), anchor(h, 1)
        relay_out[h][0, RELAY] = jnp.where(
            x == 3, first, last + terms_in[h][FROM_L + MAIN].astype(F32)
        ).astype(BF16)
        relay_out[h][1, RELAY] = jnp.where(
            x == 0, last, first + terms_in[h][FROM_R + MAIN].astype(F32)
        ).astype(BF16)
        for side in (0, 1):
            terms_relay_copy(h, side).start()

    def gather_terms(h):
        gather_sent(h)
        for side in (0, 1):
            terms_relay_copy(h, side).wait_recv()

        @pl.loop(0, RELAY)
        def _(k):
            terms_in[h][B_RR + k] = terms_relay[h][0, k]
            terms_in[h][B_RL + k] = terms_relay[h][1, k]

        @pl.loop(0, TARGETS)
        def _(t):
            total = terms_in[h][source_t[h, t * DEEP]].astype(F32)
            for k in range(1, DEEP):
                total += terms_in[h][source_t[h, t * DEEP + k]].astype(F32)
            table[h][t] = total.astype(BF16)

        def add(t, part):
            table[h][t] = (table[h][t].astype(F32) + part).astype(BF16)

        relayed = terms_relay[h][0, RELAY].astype(F32) + terms_relay[h][1, RELAY].astype(F32)

        @pl.when(x == 0)
        def _():
            add(0, anchor(h, 0) + relayed)

        @pl.when(x == NX - 1)
        def _():
            add(TARGETS - 1, anchor(h, 1) + relayed)

        @pl.when(z == NZ - 1)
        def _():
            add(0, terms_in[h][FROM_L + MAIN + 1].astype(F32))

        @pl.when(z == 0)
        def _():
            add(TARGETS - 1, terms_in[h][FROM_R + MAIN + 1].astype(F32))

        @pl.when(z > 0)
        def _():
            add((z - 1) * BPD + BPD - 1, near[h][:, :BLOCK])

        @pl.when(z < NZ - 1)
        def _():
            add((z + 1) * BPD, near[h][:, (BPD + 1) * BLOCK :])

    def sum_copy(h, s, half, right):
        row = lax.rem(z + 5 - s, NZ) if right else lax.rem(z + NZ - 5 + s, NZ)
        way = 0 if right else 1
        return to(
            z_r if right else z_l,
            table[h].at[pl.ds(row * BPD + half * HALF, HALF)],
            (sums_r if right else sums_l)[h].at[s - 1, pl.ds(half * HALF, HALF)],
            rs_send.at[h, s - 1, half, way],
            rs_recv.at[h, s - 1, half, way],
        )

    def sum_moves(s):
        return gather_moves(4 if s == 1 else 1)

    def sum_step(h, s):
        for half, right in sum_moves(s):
            if s > 1 and (half, right) in sum_moves(s - 1):
                sum_copy(h, s - 1, half, right).wait_recv()
                row = lax.rem(z + 5 - s, NZ) if right else lax.rem(z + NZ - 5 + s, NZ)
                came = (sums_r if right else sums_l)[h]

                @pl.loop(0, HALF)
                def _(b):
                    here = row * BPD + half * HALF + b
                    table[h][here] = (
                        table[h][here].astype(F32) + came[s - 2, half * HALF + b].astype(F32)
                    ).astype(BF16)

            sum_copy(h, s, half, right).start()

    def finish(h):
        for half, right in sum_moves(4):
            sum_copy(h, 4, half, right).wait_recv()

        @pl.loop(0, BPD)
        def _(b):
            total = (
                table[h][z * BPD + b].astype(F32)
                + sums_r[h][3, b].astype(F32)
                + sums_l[h][3, b].astype(F32)
                + near[h][:, pl.ds(pl.multiple_of((b + 1) * BLOCK, BLOCK), BLOCK)]
            ).astype(BF16)
            out_k[h, b] = total[0]
            out_v[h, b] = total[1]

    def drain(h):
        for s in (1, 2, 3, 4):
            for half, right in sum_moves(s):
                sum_copy(h, s, half, right).wait_send()
        for side in (0, 1):
            terms_copy(h, side).wait_send()
            terms_relay_copy(h, side).wait_send()

    gather_start(0)
    for h in range(H):
        place_own(h)
    for h in range(H):
        gather_step(h, 2)
        if h > 0:
            send_merged(h - 1)
        gather_step(h, 3)
        gather_step(h, 4)
        if h + 1 < H:
            gather_start(h + 1)
        gather_end(h)
        send_relays(h)
        if h > 1:
            compute(h - 2)
            send_terms(h - 2)
        if h > 2:
            relay_terms(h - 3)
    send_merged(H - 1)
    compute(H - 2)
    send_terms(H - 2)
    gather_terms(0)
    for s in (1, 2):
        sum_step(0, s)
    relay_terms(1)
    for s in (3, 4):
        sum_step(0, s)
    compute(H - 1)
    send_terms(H - 1)
    gather_terms(1)
    for s in (1, 2):
        sum_step(1, s)
    relay_terms(2)
    for s in (3, 4):
        sum_step(1, s)
    finish(0)
    relay_terms(3)
    gather_terms(2)
    for s in (1, 2, 3, 4):
        sum_step(2, s)
    finish(1)
    gather_terms(3)
    for s in (1, 2, 3, 4):
        sum_step(3, s)
    finish(2)
    finish(3)
    for h in range(H):
        drain(h)


def local(query, key, value, out_grad, random_links):
    def head_major(array):
        return array.reshape(BPD, BLOCK, H, HD).transpose(2, 0, 1, 3)

    def seq_major(array):
        return array.transpose(1, 2, 0, 3).reshape(BPD * BLOCK, H, HD)

    tables = slot_tables(random_links)
    kv = jnp.stack((head_major(key), head_major(value)), axis=2)
    slots = (2, BLOCK, HD)

    def per_head(*shape, dtype=BF16):
        return [pltpu.VMEM(shape, dtype) for _ in range(H)]

    dma = pltpu.SemaphoreType.DMA
    vmem = pl.BlockSpec(memory_space=pltpu.VMEM)
    smem = pl.BlockSpec(memory_space=pltpu.SMEM)
    outs = pl.pallas_call(
        kernel,
        out_shape=[jax.ShapeDtypeStruct((H, BPD, BLOCK, HD), BF16)] * 4,
        in_specs=[vmem] * 3 + [smem] * len(tables),
        out_specs=[vmem] * 4,
        scratch_shapes=[
            per_head(TARGETS, *slots),
            per_head(2, RELAYED, *slots),
            per_head(2, RELAYED, *slots),
            per_head(2, MERGED, *slots),
            per_head(RECEIVED, *slots),
            per_head(B_SIZE, *slots),
            per_head(2, RELAYED, *slots),
            per_head(4, BPD, *slots),
            per_head(4, BPD, *slots),
            per_head(2, (BPD + 2) * BLOCK, HD, dtype=F32),
            per_head(2, 2 * BLOCK, HD, dtype=F32),
            pltpu.VMEM((2, 2 * BLOCK, HD), BF16),
            pltpu.VMEM((2, (BPD + 2) * BLOCK, HD), BF16),
            pltpu.VMEM((REFS, *slots), BF16),
            dma((H, 4, 2, 2)),
            dma((H, 4, 2, 2)),
            dma((H, 2)),
            dma((H, 2)),
            dma((H, 2)),
            dma((H, 2)),
            dma((H, 2)),
            dma((H, 2)),
            dma((H, 2)),
            dma((H, 2)),
            dma((H, 4, 2, 2)),
            dma((H, 4, 2, 2)),
        ],
        compiler_params=pltpu.CompilerParams(
            collective_id=0, has_side_effects=True, vmem_limit_bytes=60 * 2**20
        ),
        cost_estimate=pl.CostEstimate(
            flops=2 * 6 * BLOCK * 8 * BLOCK * HD * H * BPD,
            bytes_accessed=4 * 2**20,
            transcendentals=H * BPD * BLOCK * 8 * BLOCK,
        ),
    )(kv, head_major(query), head_major(out_grad), *tables)
    return tuple(seq_major(array) for array in outs)


def solution(mesh):
    split = P("ctx", "head", None)
    return jax.shard_map(
        local,
        mesh=mesh,
        in_specs=(split, split, split, split, P(None, "head", None)),
        out_specs=(split, split, split, split),
        check_vma=False,
    )
```

time: 756 us -> 260 us (0.34)
  waiting for transfers between devices: 392 us -> 0 us
  Pallas kernels: 0 us -> 242 us
  local copies, waits for them, and re-layouts: 241 us -> 13.2 us
  matrix products: 43.7 us -> 0 us
  other arithmetic: 34 us -> 4.37 us
  starting transfers between devices: 27.5 us -> 0 us
  between operations: 14.5 us -> 0.79 us
    ppermute x4 -> x0, waiting for transfers between devices: 364 us -> none  [the longest x2 361 us: extended(): lax.ppermute(tail, axis, [(i, (i + 1) % count) for i in range(ends)])]
    pallas_call x0 -> x1, Pallas kernels: none -> 242 us  [local(): pl.pallas_call(kernel, out_shape=[jax.ShapeDtypeStruct((H, BPD, BLOCK, HD...]
    dot_general x29 -> x0, matrix products: 43.7 us -> none  [the longest x4 9.12 us: backward_head(): jnp.einsum('ibk,ibd->ikd', prob_rows.astype(jnp.bfloat16), grad_one, pref...]
    reshape x20 -> x6, local copies, waits for them, and re-layouts: 45 us -> 3.06 us  [the longest x1 0.84 us: slot_tables(): links.reshape(NX, NZ, BPD, H, R)]
    gather x10 -> x0, local copies, waits for them, and re-layouts: 39.8 us -> none  [the longest x2 22.7 us: serve_blocks(): chosen = jnp.take_along_axis(kv_table, wanted[:, None, :, None], axis=2)]
    squeeze x16 -> x0, local copies, waits for them, and re-layouts: 35 us -> none  [local(): lax.map(forward_head, (query_heads, widened_heads, anchor_heads, arrived,...]
    while x60 -> x0, local copies, waits for them, and re-layouts: 30.1 us -> none
    psum x2 -> x0, waiting for transfers between devices: 28.1 us -> none  [the longest x1 19.2 us: local(): lax.psum(jnp.stack((leading, trailing), axis=1).astype(jnp.bfloat16), 'ctx')]
  transfers between devices with their start and end apart: 8 -> 0, of which waited for: 5 -> 0; matrix products, arithmetic and copies ran while one was open for 2% -> 0% of each run, Pallas kernels for 0% -> 0%
where the time goes in v1:
time: 260 us
  Pallas kernels  242 us (93%)
  local copies, waits for them, and re-layouts  13.2 us (5%)
  other arithmetic  4.37 us (2%)
    pallas_call x1, Pallas kernels, local(): pl.pallas_call(kernel, out_shape=[jax.ShapeDtypeStruct((H, BPD, BLOCK, HD...  242 us
    unnamed x25, local copies, waits for them, and re-layouts  9.15 us

profile of v1, /device:TPU:16, one launch (start us, length us, event | category | flops | bytes accessed | tf_op | source)
XLA Modules:
  0.0 259.9 jit_solution(3045821389209565779)
XLA Ops:
  0.6 0.0 copy-start
  0.7 0.1 sub.114
  0.8 0.8 reshape.464
  1.7 0.3 convert_reduce_fusion.2
  2.0 0.1 copy.66
  2.1 0.1 copy.69
  2.2 0.1 copy.65
  2.3 0.1 copy.67
  2.4 0.1 copy.70
  2.5 0.7 copy.72.count_t
  3.2 0.1 lt.96
  3.2 0.1 lt.105
  3.3 0.2 copy.64
  3.5 0.1 reshape.469
  3.6 0.1 reshape.465
  3.7 0.5 convert_reduce_fusion.1
  4.2 0.1 reduce_sum.97
  4.3 0.2 convert_reduce_fusion
  4.5 0.2 select_reduce_fusion
  4.7 0.6 broadcast_add_fusion.source_t
  5.3 0.1 add_select_fusion.5
  5.4 0.1 add_select_fusion.2
  5.5 0.4 select_reduce_fusion.2
  5.9 0.7 reshape.467.relay_t
  6.5 0.0 copy-start.7
  6.5 0.2 select_reduce_fusion.1
  6.7 0.7 reshape.466.merged_t
  7.4 0.0 copy-done.7
  7.4 0.7 select_reduce_fusion.3.giver_t
  8.1 0.0 copy-done
  8.1 0.9 copy.61
  9.0 0.3 copy-done.1
  9.3 0.1 copy.59
  9.4 1.0 copy-done.2
  10.4 0.1 copy.60
  10.4 0.0 copy-start.3
  10.4 1.1 pad_maximum_fusion.kv
  11.5 0.0 copy-done.3
  11.6 0.9 copy.62
  12.4 241.6 %shard_map.84 = (bf16[4,8,64,128]{3,2,1,0:T(8,128)(2,1)}, bf16[4,8,64,128]{3,2,1,0:T(8,128)(2,1)}, bf16[4,8,64,128]{3,2,1,0:T(8,128)(2,1)}, bf16[4,8,64,128]{3,2,1,0:T(8,128)(2,1)}) custom-call(bf16[4,8,2,64,128]{4,3,2,1,0:T(8,128)(2,1)} %pad_maximum_fusion.kv, bf16[4,8,64,128]{3,2,1,0:T(8,128)(2,1)} %bitcast.47, bf16[4,8,64,128]{3,2,1,0:T(8,128)(2,1)} %bitcast.52, ...), custom_call_target="tpu_custom_call" | custom-call | flops 1610612736 | bytes 4194304 | tf_op jit(solution)/shard_map/pallas_call | solution.py:579
  254.0 0.0 copy-start.6
  254.0 2.3 copy.73
  256.3 0.0 copy-done.6
  256.3 1.2 copy.74
  257.5 0.0 copy-done.5
  257.5 1.2 copy.75
  258.7 0.0 copy-done.4
  258.7 1.2 copy.76
  (15 shorter events, 0.1 us)
Async XLA Ops:
  0.6 7.5 %copy-start = (bf16[512,4,128]{2,1,0:T(4,128)(2,1)S(1)}, bf16[512,4,128]{2,1,0:T(4,128)(2,1)}, u32[]{:S(2)}) copy-start(bf16[512,4,128]{2,1,0:T(4,128)(2,1)} %param.5) | copy-start | bytes 1572868
  6.5 0.9 copy-start.7
  8.1 1.2 copy-start.1
  9.3 1.0 copy-start.2
  10.4 1.1 copy-start.3
  254.0 2.3 copy-start.6
  256.3 1.2 copy-start.5
  257.5 1.2 copy-start.4

commit v2 on v1

v2 whole, which is shorter than its diff:
```python
import math

import jax
import jax.numpy as jnp
from jax import lax
from jax.experimental import pallas as pl
from jax.experimental.pallas import tpu as pltpu
from jax.sharding import PartitionSpec as P

BLOCK = 64
HD = 128
NX = 4
NZ = 8
BPD = 8
HALF = BPD // 2
H = 4
R = 3
REFS = BPD * R
TARGETS = NZ * BPD
MAIN = 16
RELAY = 8
UNITS = 2 * H
FROM_R, FROM_L, OWN = 0, MAIN, 2 * MAIN
RECEIVED = OWN + MAIN
B_RR = 2 * MAIN
B_RL = B_RR + RELAY
B_OWN = B_RL + RELAY
B_ZERO = B_OWN + MAIN
B_SIZE = B_ZERO + 1
PIECES = 2
DEEP = 8
F32 = jnp.float32
BF16 = jnp.bfloat16
MESH = pl.DeviceIdType.MESH
SCALE = 1.0 / math.sqrt(HD)


def slot_tables(links):
    ctx = lax.axis_index("ctx")
    x, z = ctx // NZ, ctx % NZ
    row = lax.dynamic_slice_in_dim(links.reshape(NX, NZ, BPD, H, R), z, 1, 1)[:, 0]
    named = row.transpose(2, 0, 1, 3).reshape(H, NX, REFS)
    planes = jnp.arange(NX, dtype=jnp.int32)
    away = (named // TARGETS - planes[None, :, None]) % NX
    target = named % TARGETS
    entry = jnp.arange(REFS, dtype=jnp.int32)
    before = entry[None, :] < entry[:, None]
    rank = jnp.sum(
        ((away[..., None, :] == away[..., :, None]) & before).astype(jnp.int32), axis=-1
    )
    n_r = jnp.sum((away == 1).astype(jnp.int32), axis=-1)
    n_o = jnp.sum((away == 2).astype(jnp.int32), axis=-1)
    n_l = jnp.sum((away == 3).astype(jnp.int32), axis=-1)
    by_right = jnp.minimum(n_o, jnp.minimum(RELAY, MAIN - n_r))[..., None]
    right_way = rank < by_right
    place = jnp.where(
        away == 0,
        OWN + rank,
        jnp.where(
            away == 1,
            FROM_R + rank,
            jnp.where(
                away == 3,
                FROM_L + rank,
                jnp.where(
                    right_way,
                    FROM_R + n_r[..., None] + rank,
                    FROM_L + n_l[..., None] + rank - by_right,
                ),
            ),
        ),
    )
    relay_rank = jnp.where(right_way, rank, rank - by_right)
    code = jnp.where(away == 2, TARGETS + relay_rank, target)
    spots = jnp.arange(RECEIVED, dtype=jnp.int32)
    hit = place[..., None] == spots
    merged = jnp.sum(jnp.where(hit, code[..., None], 0), axis=2)
    relay_place = jnp.where(away == 2, jnp.where(right_way, 0, RELAY) + relay_rank, -1)
    relays = jnp.sum(
        jnp.where(
            relay_place[..., None] == jnp.arange(2 * RELAY, dtype=jnp.int32), target[..., None], 0
        ),
        axis=2,
    )
    own_place = lax.dynamic_slice_in_dim(place, x, 1, 1)[:, 0]
    giver = jnp.sum(
        jnp.where(own_place[..., None] == spots, entry[None, :, None], 0), axis=1
    )
    landing = jnp.where(
        away == 0,
        B_OWN + rank,
        jnp.where(
            away == 1,
            FROM_L + rank,
            jnp.where(
                away == 3, FROM_R + rank, jnp.where(right_way, B_RL, B_RR) + relay_rank
            ),
        ),
    ).reshape(H, NX * REFS)
    here = jnp.where(named // TARGETS == x, target, -1).reshape(H, NX * REFS)
    every = jnp.arange(NX * REFS, dtype=jnp.int32)
    same = (here[:, None, :] == here[:, :, None]) & (every[None, :] < every[:, None])
    depth = jnp.sum(same.astype(jnp.int32), axis=-1)
    cell = jnp.where(here >= 0, here * DEEP + depth, -1)
    cells = jnp.arange(TARGETS * DEEP, dtype=jnp.int32)
    sources = B_ZERO + jnp.sum(
        jnp.where(cell[:, :, None] == cells, landing[:, :, None] - B_ZERO, 0), axis=1
    )
    counts = jnp.stack((n_r, n_l), axis=-1).reshape(H, 2 * NX)
    return (
        merged.reshape(H, NX * RECEIVED),
        relays.reshape(H, NX * 2 * RELAY),
        own_place,
        giver,
        counts,
        sources,
    )


ORDER = (
    ("GS", 0), ("PO", 0), ("PO", 1), ("PO", 2), ("PO", 3), ("G", 0, 2, 0), ("G", 0, 2, 1),
    ("G", 0, 3, 0), ("G", 0, 3, 1), ("GS", 1), ("G", 0, 4, 0), ("G", 0, 4, 1), ("G", 1, 2, 0),
    ("G", 1, 2, 1), ("GE", 0), ("SR", 0), ("G", 1, 3, 0), ("G", 1, 3, 1), ("GS", 2),
    ("G", 1, 4, 0), ("SM", 0), ("G", 1, 4, 1), ("G", 2, 2, 0), ("G", 2, 2, 1), ("GE", 1),
    ("SR", 1), ("G", 2, 3, 0), ("G", 2, 3, 1), ("GS", 3), ("G", 2, 4, 0), ("SM", 1),
    ("G", 2, 4, 1), ("G", 3, 2, 0), ("G", 3, 2, 1), ("GE", 2), ("SR", 2), ("G", 3, 3, 0),
    ("G", 3, 3, 1), ("C", 0, 0), ("SM", 2), ("G", 3, 4, 0), ("G", 3, 4, 1), ("C", 0, 1), ("ST", 0),
    ("GE", 3), ("SR", 3), ("ST", 1), ("GS", 4), ("G", 4, 2, 0), ("G", 4, 2, 1), ("G", 4, 3, 0),
    ("G", 4, 3, 1), ("GS", 5), ("RT", 0), ("G", 4, 4, 0), ("G", 4, 4, 1), ("SM", 3),
    ("G", 5, 2, 0), ("G", 5, 2, 1), ("GE", 4), ("SR", 4), ("G", 5, 3, 0), ("RT", 1),
    ("G", 5, 3, 1), ("GS", 6), ("G", 5, 4, 0), ("L", 0), ("R", 0, 1), ("SS", 0), ("R", 0, 2),
    ("G", 5, 4, 1), ("R", 0, 3), ("R", 0, 4), ("R", 0, 5), ("G", 6, 2, 0), ("G", 6, 2, 1),
    ("S", 0, 2, 0), ("S", 0, 2, 1), ("C", 1, 0), ("SM", 4), ("G", 6, 3, 0), ("G", 6, 3, 1),
    ("GE", 5), ("SR", 5), ("S", 0, 3, 0), ("C", 1, 1), ("S", 0, 3, 1), ("L", 1), ("ST", 2),
    ("G", 6, 4, 0), ("G", 6, 4, 1), ("R", 1, 1), ("SS", 1), ("R", 1, 2), ("R", 1, 3),
    ("S", 0, 4, 0), ("R", 1, 4), ("R", 1, 5), ("ST", 3), ("S", 0, 4, 1), ("GS", 7), ("GE", 6),
    ("SR", 6), ("SM", 5), ("S", 1, 2, 0), ("S", 1, 2, 1), ("F", 0), ("G", 7, 2, 0), ("RT", 2),
    ("G", 7, 2, 1), ("S", 1, 3, 0), ("S", 1, 3, 1), ("G", 7, 3, 0), ("RT", 3), ("G", 7, 3, 1),
    ("S", 1, 4, 0), ("SM", 6), ("S", 1, 4, 1), ("G", 7, 4, 0), ("G", 7, 4, 1), ("C", 2, 0),
    ("L", 2), ("F", 1), ("R", 2, 1), ("SS", 2), ("R", 2, 2), ("R", 2, 3), ("R", 2, 4), ("R", 2, 5),
    ("GE", 7), ("SR", 7), ("L", 3), ("R", 3, 1), ("SS", 3), ("R", 3, 2), ("R", 3, 3),
    ("S", 2, 2, 0), ("S", 2, 2, 1), ("R", 3, 4), ("R", 3, 5), ("C", 2, 1), ("S", 2, 3, 0),
    ("S", 3, 2, 0), ("S", 2, 3, 1), ("S", 3, 2, 1), ("ST", 4), ("ST", 5), ("SM", 7),
    ("S", 2, 4, 0), ("S", 3, 3, 0), ("S", 2, 4, 1), ("S", 3, 3, 1), ("RT", 4), ("S", 3, 4, 0),
    ("F", 2), ("S", 3, 4, 1), ("RT", 5), ("F", 3), ("C", 3, 0), ("L", 4), ("R", 4, 1), ("SS", 4),
    ("R", 4, 2), ("R", 4, 3), ("R", 4, 4), ("R", 4, 5), ("C", 3, 1), ("S", 4, 2, 0),
    ("S", 4, 2, 1), ("L", 5), ("ST", 6), ("R", 5, 1), ("SS", 5), ("R", 5, 2), ("R", 5, 3),
    ("R", 5, 4), ("R", 5, 5), ("ST", 7), ("S", 4, 3, 0), ("S", 4, 3, 1), ("S", 5, 2, 0),
    ("S", 5, 2, 1), ("S", 4, 4, 0), ("RT", 6), ("S", 4, 4, 1), ("S", 5, 3, 0), ("S", 5, 3, 1),
    ("RT", 7), ("F", 4), ("S", 5, 4, 0), ("L", 6), ("R", 6, 1), ("SS", 6), ("S", 5, 4, 1),
    ("R", 6, 2), ("R", 6, 3), ("R", 6, 4), ("R", 6, 5), ("L", 7), ("R", 7, 1), ("SS", 7),
    ("R", 7, 2), ("S", 6, 2, 0), ("S", 6, 2, 1), ("R", 7, 3), ("R", 7, 4), ("F", 5), ("R", 7, 5),
    ("S", 7, 2, 0), ("S", 7, 2, 1), ("S", 6, 3, 0), ("S", 6, 3, 1), ("S", 7, 3, 0), ("S", 7, 3, 1),
    ("S", 6, 4, 0), ("S", 6, 4, 1), ("S", 7, 4, 0), ("S", 7, 4, 1), ("F", 6), ("F", 7),
)


def kernel(
    kv,
    query,
    grad,
    merged_t,
    relay_t,
    place_t,
    giver_t,
    count_t,
    source_t,
    out_o,
    out_q,
    out_k,
    out_v,
    table,
    relay_out,
    relay_in,
    merged_out,
    received,
    terms_in,
    terms_relay,
    sums_r,
    sums_l,
    near,
    anchor_acc,
    anchor_in,
    part_out,
    part_in,
    edge_out,
    edge_in,
    edge_part_out,
    edge_part_in,
    anchor_kv,
    wide,
    terms,
    ag_sem,
    rs_sem,
    x_sem,
    anchor_sem,
    part_sem,
    edge_sem,
):
    ctx = lax.axis_index("ctx")
    x, z = ctx // NZ, ctx % NZ
    z_r = x * NZ + lax.rem(z + 1, NZ)
    z_l = x * NZ + lax.rem(z + NZ - 1, NZ)
    p_r = lax.rem(x + 1, NX)
    p_l = lax.rem(x + NX - 1, NX)
    p_o = lax.rem(x + 2, NX)
    x_r = p_r * NZ + z
    x_l = p_l * NZ + z
    outer = (x == 0) | (x == NX - 1)
    inner = (x == 1) | (x == NX - 2)
    rim = (z == 0) | (z == NZ - 1)
    beyond = lax.rem(jnp.where(z == 0, ctx + NX * NZ - 1, ctx + 1), NX * NZ)

    def to(device, src, dst, sems):
        return pltpu.make_async_remote_copy(
            src_ref=src,
            dst_ref=dst,
            send_sem=sems.at[0],
            recv_sem=sems.at[1],
            device_id={"ctx": device},
            device_id_type=MESH,
        )

    barrier = pltpu.get_barrier_semaphore()

    def greet(device):
        pl.semaphore_signal(barrier, inc=1, device_id={"ctx": device}, device_id_type=MESH)

    for device in (z_r, z_l, x_r, x_l):
        greet(device)

    @pl.when(rim)
    def _():
        greet(beyond)

    pl.semaphore_wait(barrier, 4 + rim.astype(jnp.int32))

    def gather_copy(u, s, half, right):
        row = lax.rem(z + NZ - (s - 1), NZ) if right else lax.rem(z + s - 1, NZ)
        cut = pl.ds(row * BPD + half * HALF, HALF)
        src = kv.at[u, pl.ds(half * HALF, HALF)] if s == 1 else table[u].at[cut]
        way = 0 if right else 1
        return to(z_r if right else z_l, src, table[u].at[cut], ag_sem.at[u, s - 1, half, way])

    def moves(s):
        return [
            (half, right)
            for half in (0, 1)
            for right in (True, False)
            if s < 4 or right == (half == 0)
        ]

    def gather_start(u):
        for half, right in moves(1):
            gather_copy(u, 1, half, right).start()

    def gather_step(u, s, half):
        for right in (True, False):
            gather_copy(u, s - 1, half, right).wait_recv()
            if (half, right) in moves(s):
                gather_copy(u, s, half, right).start()

    def gather_end(u):
        for half, right in moves(4):
            gather_copy(u, 4, half, right).wait_recv()

    def gather_sent(u):
        for s in (1, 2, 3, 4):
            for half, right in moves(s):
                gather_copy(u, s, half, right).wait_send()

    def place_own(h):
        for p in (0, 1):

            @pl.loop(0, BPD)
            def _(b):
                table[2 * h + p][z * BPD + b] = kv[2 * h + p, b]

    def edge_copy():
        return to(beyond, edge_out, edge_in, edge_sem.at[UNITS])

    def send_edges():
        @pl.when(rim)
        def _():
            @pl.loop(0, UNITS)
            def _(u):
                edge_out[u] = kv[u, jnp.where(z == 0, 0, BPD - 1)]

            edge_copy().start()

    def relay_copy(u, side):
        return to(
            (x_r, x_l)[side], relay_out[u].at[side], relay_in[u].at[1 - side], x_sem.at[0, u, side]
        )

    def merged_copy(u, side):
        return to(
            (x_r, x_l)[side],
            merged_out[u].at[side],
            received[u].at[pl.ds((FROM_L, FROM_R)[side], MAIN)],
            x_sem.at[1, u, side],
        )

    def anchor_copy(u, side):
        return to(
            (x_r, x_l)[side],
            table[u].at[jnp.where(x == 0, 0, TARGETS - 1)],
            anchor_in.at[u, 0],
            anchor_sem.at[u, side],
        )

    def anchor_arrived(u):
        @pl.when((x == 0) | (x == 1))
        def _():
            anchor_copy(u, 0).wait_recv()

        @pl.when((x == 2) | (x == 3))
        def _():
            anchor_copy(u, 1).wait_recv()

    def anchor_pass(u):
        return to(
            jnp.where(x == 1, x_r, x_l), anchor_in.at[u, 0], anchor_in.at[u, 1], anchor_sem.at[u, 2]
        )

    def send_relays(u):
        h = u // 2

        @pl.when(outer)
        def _():
            for side in (0, 1):
                anchor_copy(u, side).start()

        @pl.loop(0, RELAY)
        def _(k):
            relay_out[u][0, k] = table[u][relay_t[h, p_o * 2 * RELAY + RELAY + k]]
            relay_out[u][1, k] = table[u][relay_t[h, p_o * 2 * RELAY + k]]

        for side in (0, 1):
            relay_copy(u, side).start()

        @pl.loop(0, MAIN)
        def _(k):
            received[u][OWN + k] = table[u][merged_t[h, x * RECEIVED + OWN + k]]

    def send_merged(u):
        h = u // 2
        for side in (0, 1):
            relay_copy(u, side).wait_recv()

        @pl.loop(0, MAIN)
        def _(k):
            for side, plane, first, back in ((0, p_r, FROM_L, 1), (1, p_l, FROM_R, 0)):
                code = merged_t[h, plane * RECEIVED + first + k]
                direct = table[u][jnp.minimum(code, TARGETS - 1)]
                passed = relay_in[u][back, jnp.maximum(code - TARGETS, 0)]
                merged_out[u][side, k] = jnp.where(code < TARGETS, direct, passed)

        for side in (0, 1):
            merged_copy(u, side).start()
        anchor_arrived(u)

        @pl.when(inner)
        def _():
            anchor_pass(u).start()

    def lay_keys(h):
        for p in (0, 1):
            u = 2 * h + p
            for side in (0, 1):
                merged_copy(u, side).wait_recv()

            @pl.when(inner)
            def _():
                anchor_pass(u).wait_recv()

            row_above = lax.rem(z + NZ - 1, NZ) * BPD + BPD - 1
            row_below = lax.rem(z + 1, NZ) * BPD
            wide[p, 0:BLOCK] = jnp.where(z > 0, table[u][row_above], edge_in[u])
            wide[p, BLOCK * (BPD + 1) :] = jnp.where(z < NZ - 1, table[u][row_below], edge_in[u])
            for b in range(BPD):
                wide[p, BLOCK * (b + 1) : BLOCK * (b + 2)] = kv[u, b]
            came, passed = anchor_in[u, 0], anchor_in[u, 1]
            anchor_kv[p, :BLOCK] = jnp.where(x == 0, table[u][0], jnp.where(x == 2, passed, came))
            anchor_kv[p, BLOCK:] = jnp.where(
                x == 3, table[u][TARGETS - 1], jnp.where(x == 1, passed, came)
            )
        near[h][...] = jnp.zeros_like(near[h])
        anchor_acc[h][...] = jnp.zeros_like(anchor_acc[h])

    def compute(h, piece):
        if piece == 0:
            if h == 0:

                @pl.when(rim)
                def _():
                    edge_copy().wait_recv()

            lay_keys(h)
        column = lax.broadcasted_iota(jnp.int32, (1, 8 * BLOCK), 1)

        @pl.loop(piece * BPD // PIECES, (piece + 1) * BPD // PIECES)
        def _(i):
            rows = pl.ds(pl.multiple_of(i * BLOCK, BLOCK), 3 * BLOCK)
            spots = [place_t[h, i * R + r] for r in range(R)]
            keys, values = (
                jnp.concatenate(
                    [wide[p, rows], anchor_kv[p]] + [received[2 * h + p][s] for s in spots], axis=0
                )
                for p in (0, 1)
            )
            q, g = query[h, i], grad[h, i]
            block = ctx * BPD + i
            low = jnp.where(block == 0, BLOCK, 0)
            cut = jnp.where(block == NX * NZ * BPD - 1, 2 * BLOCK, 3 * BLOCK)
            masked = (column < low) | ((column >= cut) & (column < 3 * BLOCK))
            contract_last = (((1,), (1,)), ((), ()))
            contract_first = (((0,), (0,)), ((), ()))
            scores = lax.dot_general(q, keys, contract_last, preferred_element_type=F32) * SCALE
            scores = jnp.where(masked, -1e30, scores)
            powers = jnp.exp(scores - jnp.max(scores, axis=-1, keepdims=True))
            probs = powers * (1.0 / jnp.sum(powers, axis=-1, keepdims=True))
            low_probs = probs.astype(BF16)
            attended = jnp.dot(low_probs, values, preferred_element_type=F32).astype(BF16)
            out_o[h, i] = attended
            delta = jnp.sum(g.astype(F32) * attended.astype(F32), axis=-1, keepdims=True)
            grad_probs = lax.dot_general(g, values, contract_last, preferred_element_type=F32)
            grad_scores = (probs * (grad_probs - delta)).astype(BF16)
            out_q[h, i] = (
                jnp.dot(grad_scores, keys, preferred_element_type=F32) * SCALE
            ).astype(BF16)
            key_part = (
                lax.dot_general(grad_scores, q, contract_first, preferred_element_type=F32) * SCALE
            )
            value_part = lax.dot_general(
                low_probs, g, contract_first, preferred_element_type=F32
            )
            for p, part in ((0, key_part), (1, value_part)):
                near[h][p, rows] += part[: 3 * BLOCK]
                anchor_acc[h][p] += part[3 * BLOCK : 5 * BLOCK]
                for r in range(R):
                    terms[p, i * R + r] = part[(5 + r) * BLOCK : (6 + r) * BLOCK].astype(BF16)

    def terms_copy(u, side):
        return to(
            (x_r, x_l)[side],
            merged_out[u].at[side],
            terms_in[u].at[pl.ds((FROM_L, FROM_R)[side], MAIN)],
            x_sem.at[2, u, side],
        )

    def terms_relay_copy(u, side):
        return to(
            (x_r, x_l)[side], relay_out[u].at[side], terms_relay[u].at[1 - side],
            x_sem.at[3, u, side],
        )

    def part_first(u):
        return to(
            jnp.where(x == 1, x_r, x_l), part_out.at[u, 0], part_in.at[u, 0], part_sem.at[u, 0]
        )

    def part_second(u, side):
        return to(
            (x_r, x_l)[side], part_out.at[u, 1], part_in.at[u, 1 + side], part_sem.at[u, 1 + side]
        )

    def leftward():
        return (x == 0) | (x == 1)

    def edge_part_copy(u):
        return to(beyond, edge_part_out.at[u], edge_part_in.at[u], edge_sem.at[u])

    def anchor(u, which):
        return anchor_acc[u // 2][u % 2, which * BLOCK : (which + 1) * BLOCK]

    def near_rows(u, b):
        return near[u // 2][u % 2, (b + 1) * BLOCK : (b + 2) * BLOCK]

    def send_terms(u):
        h, p = u // 2, u % 2
        for side in (0, 1):
            merged_copy(u, side).wait_send()

        @pl.loop(0, MAIN)
        def _(k):
            merged_out[u][0, k] = terms[p, giver_t[h, FROM_R + k]]
            merged_out[u][1, k] = terms[p, giver_t[h, FROM_L + k]]
            terms_in[u][B_OWN + k] = terms[p, giver_t[h, OWN + k]]

        for side in (0, 1):
            terms_copy(u, side).start()
        terms_in[u][B_ZERO] = jnp.zeros((BLOCK, HD), BF16)

        @pl.when(inner)
        def _():
            part_out[u, 0] = jnp.where(x == 1, anchor(u, 1), anchor(u, 0)).astype(BF16)
            part_first(u).start()

        @pl.when(rim)
        def _():
            edge_part_out[u] = jnp.where(z == 0, near_rows(u, -1), near_rows(u, BPD)).astype(BF16)
            edge_part_copy(u).start()

    def relay_terms(u):
        h = u // 2
        for side in (0, 1):
            relay_copy(u, side).wait_send()
            terms_copy(u, side).wait_recv()

        @pl.loop(0, RELAY)
        def _(k):
            from_left = count_t[h, p_l * 2] + k
            from_right = count_t[h, p_r * 2 + 1] + k
            relay_out[u][0, k] = terms_in[u][FROM_L + jnp.minimum(from_left, MAIN - 1)]
            relay_out[u][1, k] = terms_in[u][FROM_R + jnp.minimum(from_right, MAIN - 1)]

        for side in (0, 1):
            terms_relay_copy(u, side).start()

        @pl.when(inner)
        def _():
            part_first(u).wait_recv()
            mine = jnp.where(x == 1, anchor(u, 0), anchor(u, 1))
            part_out[u, 1] = (mine + part_in[u, 0].astype(F32)).astype(BF16)

        @pl.when(outer)
        def _():
            part_out[u, 1] = jnp.where(x == 0, anchor(u, 1), anchor(u, 0)).astype(BF16)

        @pl.when(leftward())
        def _():
            part_second(u, 1).start()

        @pl.when(jnp.logical_not(leftward()))
        def _():
            part_second(u, 0).start()

    def land(u):
        gather_sent(u)

        @pl.when(outer)
        def _():
            for side in (0, 1):
                anchor_copy(u, side).wait_send()
                part_second(u, side).wait_recv()

        for side in (0, 1):
            terms_relay_copy(u, side).wait_recv()

        @pl.loop(0, RELAY)
        def _(k):
            terms_in[u][B_RR + k] = terms_relay[u][0, k]
            terms_in[u][B_RL + k] = terms_relay[u][1, k]

    def rows(u, group):
        h = u // 2
        for away in {1: (4,), 2: (3, 5), 3: (2, 6), 4: (1, 7), 5: (0,)}[group]:
            row = lax.rem(z + away, NZ)

            @pl.loop(0, BPD)
            def _(b):
                t = row * BPD + b
                total = terms_in[u][source_t[h, t * DEEP]].astype(F32)
                for k in range(1, DEEP):
                    total += terms_in[u][source_t[h, t * DEEP + k]].astype(F32)
                table[u][t] = total.astype(BF16)

            def add(t, part):
                table[u][t] = (table[u][t].astype(F32) + part).astype(BF16)

            def both():
                return part_in[u, 1].astype(F32) + part_in[u, 2].astype(F32)

            @pl.when((x == 0) & (row == 0))
            def _():
                add(0, anchor(u, 0) + both())

            @pl.when((x == NX - 1) & (row == NZ - 1))
            def _():
                add(TARGETS - 1, anchor(u, 1) + both())

            if away == NZ - 1:

                @pl.when(z > 0)
                def _():
                    add(row * BPD + BPD - 1, near_rows(u, -1))

            if away == 1:

                @pl.when(z < NZ - 1)
                def _():
                    add(row * BPD, near_rows(u, BPD))

    def sum_copy(u, s, half, right):
        row = lax.rem(z + 5 - s, NZ) if right else lax.rem(z + NZ - 5 + s, NZ)
        way = 0 if right else 1
        return to(
            z_r if right else z_l,
            table[u].at[pl.ds(row * BPD + half * HALF, HALF)],
            (sums_r if right else sums_l)[u].at[s - 1, pl.ds(half * HALF, HALF)],
            rs_sem.at[u, s - 1, half, way],
        )

    def sum_moves(s):
        return moves(4 if s == 1 else 1)

    def sum_start(u):
        for half, right in sum_moves(1):
            sum_copy(u, 1, half, right).start()

    def sum_step(u, s, half):
        for right in (True, False):
            if (half, right) in sum_moves(s - 1):
                sum_copy(u, s - 1, half, right).wait_recv()
                row = lax.rem(z + 5 - s, NZ) if right else lax.rem(z + NZ - 5 + s, NZ)
                came = (sums_r if right else sums_l)[u]

                @pl.loop(0, HALF)
                def _(b):
                    here = row * BPD + half * HALF + b
                    table[u][here] = (
                        table[u][here].astype(F32) + came[s - 2, half * HALF + b].astype(F32)
                    ).astype(BF16)

            sum_copy(u, s, half, right).start()

    def finish(u):
        h, p = u // 2, u % 2
        for half, right in sum_moves(4):
            sum_copy(u, 4, half, right).wait_recv()

        @pl.when(rim)
        def _():
            edge_part_copy(u).wait_recv()
            lone = pl.ds(pl.multiple_of(jnp.where(z == 0, 1, BPD) * BLOCK, BLOCK), BLOCK)
            near[h][p, lone] += edge_part_in[u].astype(F32)

        @pl.loop(0, BPD)
        def _(b):
            total = (
                table[u][z * BPD + b].astype(F32)
                + sums_r[u][3, b].astype(F32)
                + sums_l[u][3, b].astype(F32)
                + near[h][p, pl.ds(pl.multiple_of((b + 1) * BLOCK, BLOCK), BLOCK)]
            )
            (out_k, out_v)[p][h, b] = total.astype(BF16)

    def drain(u):
        for s in (1, 2, 3, 4):
            for half, right in sum_moves(s):
                sum_copy(u, s, half, right).wait_send()
        for side in (0, 1):
            terms_copy(u, side).wait_send()
            terms_relay_copy(u, side).wait_send()

        @pl.when(inner)
        def _():
            anchor_pass(u).wait_send()
            part_first(u).wait_send()

        @pl.when(leftward())
        def _():
            part_second(u, 1).wait_send()

        @pl.when(jnp.logical_not(leftward()))
        def _():
            part_second(u, 0).wait_send()

        @pl.when(rim)
        def _():
            edge_part_copy(u).wait_send()

    steps = {
        "GS": gather_start,
        "G": gather_step,
        "GE": gather_end,
        "PO": place_own,
        "SR": send_relays,
        "SM": send_merged,
        "C": compute,
        "ST": send_terms,
        "RT": relay_terms,
        "L": land,
        "R": rows,
        "SS": sum_start,
        "S": sum_step,
        "F": finish,
    }
    send_edges()
    for name, *where in ORDER:
        steps[name](*where)
    for u in range(UNITS):
        drain(u)

    @pl.when(rim)
    def _():
        edge_copy().wait_send()


def local(query, key, value, out_grad, random_links):
    def head_major(array):
        return array.reshape(BPD, BLOCK, H, HD).transpose(2, 0, 1, 3)

    def seq_major(array):
        return array.transpose(1, 2, 0, 3).reshape(BPD * BLOCK, H, HD)

    tables = slot_tables(random_links)
    kv = jnp.stack((head_major(key), head_major(value)), axis=1).reshape(UNITS, BPD, BLOCK, HD)
    block = (BLOCK, HD)

    def per(count, *shape, dtype=BF16):
        return [pltpu.VMEM(shape, dtype) for _ in range(count)]

    dma = pltpu.SemaphoreType.DMA
    vmem = pl.BlockSpec(memory_space=pltpu.VMEM)
    smem = pl.BlockSpec(memory_space=pltpu.SMEM)
    outs = pl.pallas_call(
        kernel,
        out_shape=[jax.ShapeDtypeStruct((H, BPD, BLOCK, HD), BF16)] * 4,
        in_specs=[vmem] * 3 + [smem] * len(tables),
        out_specs=[vmem] * 4,
        scratch_shapes=[
            per(UNITS, TARGETS, *block),
            per(UNITS, 2, RELAY, *block),
            per(UNITS, 2, RELAY, *block),
            per(UNITS, 2, MAIN, *block),
            per(UNITS, RECEIVED, *block),
            per(UNITS, B_SIZE, *block),
            per(UNITS, 2, RELAY, *block),
            per(UNITS, 4, BPD, *block),
            per(UNITS, 4, BPD, *block),
            per(H, 2, (BPD + 2) * BLOCK, HD, dtype=F32),
            per(H, 2, 2 * BLOCK, HD, dtype=F32),
            pltpu.VMEM((UNITS, 2, *block), BF16),
            pltpu.VMEM((UNITS, 2, *block), BF16),
            pltpu.VMEM((UNITS, 3, *block), BF16),
            pltpu.VMEM((UNITS, *block), BF16),
            pltpu.VMEM((UNITS, *block), BF16),
            pltpu.VMEM((UNITS, *block), BF16),
            pltpu.VMEM((UNITS, *block), BF16),
            pltpu.VMEM((2, 2 * BLOCK, HD), BF16),
            pltpu.VMEM((2, (BPD + 2) * BLOCK, HD), BF16),
            pltpu.VMEM((2, REFS, *block), BF16),
            dma((UNITS, 4, 2, 2, 2)),
            dma((UNITS, 4, 2, 2, 2)),
            dma((4, UNITS, 2, 2)),
            dma((UNITS, 3, 2)),
            dma((UNITS, 3, 2)),
            dma((UNITS + 1, 2)),
        ],
        compiler_params=pltpu.CompilerParams(
            collective_id=0, has_side_effects=True, vmem_limit_bytes=60 * 2**20
        ),
        cost_estimate=pl.CostEstimate(
            flops=2 * 6 * BLOCK * 8 * BLOCK * HD * H * BPD,
            bytes_accessed=4 * 2**20,
            transcendentals=H * BPD * BLOCK * 8 * BLOCK,
        ),
    )(kv, head_major(query), head_major(out_grad), *tables)
    return tuple(seq_major(array) for array in outs)


def solution(mesh):
    split = P("ctx", "head", None)
    return jax.shard_map(
        local,
        mesh=mesh,
        in_specs=(split, split, split, split, P(None, "head", None)),
        out_specs=(split, split, split, split),
        check_vma=False,
    )
```

time: 260 us -> 229 us (0.88)
  Pallas kernels: 242 us -> 210 us
    pallas_call x1, Pallas kernels: 242 us -> 210 us  [local(): pl.pallas_call(kernel, out_shape=[jax.ShapeDtypeStruct((H, BPD, BLOCK, HD...]
    unnamed x25 -> x23, local copies, waits for them, and re-layouts: 9.15 us -> 8.52 us
where the time goes in v2:
time: 229 us; the launch traced here: 228 us
  Pallas kernels  210 us (92%)
  local copies, waits for them, and re-layouts  12.8 us (6%)
  other arithmetic  4.37 us (2%)
    pallas_call x1, Pallas kernels, local(): pl.pallas_call(kernel, out_shape=[jax.ShapeDtypeStruct((H, BPD, BLOCK, HD...  210 us
    unnamed x23, local copies, waits for them, and re-layouts  8.52 us

profile of v2, /device:TPU:16, one launch (start us, length us, event | category | flops | bytes accessed | tf_op | source)
XLA Modules:
  0.0 227.8 jit_solution(14607702773566328190)
XLA Ops:
  0.6 0.0 copy-start
  0.7 0.1 sub.114
  0.8 0.8 reshape.468
  1.7 0.3 convert_reduce_fusion.2
  2.0 0.1 copy.66
  2.1 0.1 copy.69
  2.2 0.1 copy.65
  2.3 0.1 copy.67
  2.4 0.1 copy.70
  2.5 0.7 copy.72.count_t
  3.2 0.1 lt.96
  3.2 0.1 lt.105
  3.3 0.2 copy.64
  3.5 0.1 reshape.473
  3.6 0.1 reshape.469
  3.7 0.5 convert_reduce_fusion.1
  4.2 0.1 reduce_sum.97
  4.3 0.2 convert_reduce_fusion
  4.5 0.2 select_reduce_fusion
  4.7 0.6 broadcast_add_fusion.source_t
  5.3 0.1 add_select_fusion.5
  5.4 0.1 add_select_fusion.2
  5.5 0.4 select_reduce_fusion.2
  5.9 0.7 reshape.471.relay_t
  6.5 0.0 copy-start.7
  6.5 0.2 select_reduce_fusion.1
  6.7 0.7 reshape.470.merged_t
  7.4 0.0 copy-done.7
  7.4 0.7 select_reduce_fusion.3.giver_t
  8.1 0.0 copy-done
  8.1 0.0 copy-start.1
  8.1 0.9 copy.61
  9.0 0.3 copy-done.1
  9.3 0.0 copy-start.5
  9.3 0.9 copy.62
  10.2 0.3 copy-done.5
  10.5 0.2 copy-done.6
  10.7 0.2 copy_bitcast_fusion
  11.0 1.1 pad_maximum_fusion
  12.0 209.9 %shard_map.84 = (bf16[4,8,64,128]{3,2,1,0:T(8,128)(2,1)}, bf16[4,8,64,128]{3,2,1,0:T(8,128)(2,1)}, bf16[4,8,64,128]{3,2,1,0:T(8,128)(2,1)}, bf16[4,8,64,128]{3,2,1,0:T(8,128)(2,1)}) custom-call(bf16[8,8,64,128]{3,2,1,0:T(8,128)(2,1)} %bitcast.46, bf16[4,8,64,128]{3,2,1,0:T(8,128)(2,1)} %bitcast.47, bf16[4,8,64,128]{3,2,1,0:T(8,128)(2,1)} %bitcast.48, ...), custom_call_target="tpu_custom_call" | custom-call | flops 1610612736 | bytes 4194304 | tf_op jit(solution)/shard_map/pallas_call | solution.py:718
  221.9 0.0 copy-start.4
  221.9 2.3 %copy.73 = bf16[512,4,128]{2,1,0:T(4,128)(2,1)} copy(bf16[512,4,128]{2,0,1:T(8,128)(2,1)} %bitcast.52) | data formatting | bytes 1048576
  224.2 0.0 copy-done.4
  224.2 1.2 copy.74
  225.4 0.0 copy-done.3
  225.4 1.2 copy.75
  226.6 0.0 copy-done.2
  226.6 1.2 copy.76
  (14 shorter events, 0.1 us)
Async XLA Ops:
  0.6 7.5 %copy-start = (bf16[512,4,128]{2,1,0:T(4,128)(2,1)S(1)}, bf16[512,4,128]{2,1,0:T(4,128)(2,1)}, u32[]{:S(2)}) copy-start(bf16[512,4,128]{2,1,0:T(4,128)(2,1)} %param.5) | copy-start | bytes 1572868
  6.5 0.9 copy-start.7
  8.1 1.2 copy-start.1
  9.3 1.2 copy-start.5
  9.3 1.4 copy-start.6
  221.9 2.3 %copy-start.4 = (bf16[4,8,64,128]{3,2,1,0:T(8,128)(2,1)S(1)}, bf16[4,8,64,128]{3,2,1,0:T(8,128)(2,1)}, u32[]{:S(2)}) copy-start(bf16[4,8,64,128]{3,2,1,0:T(8,128)(2,1)} %get-tuple-element.9) | copy-start | bytes 1572868
  224.2 1.2 copy-start.3
  225.4 1.2 copy-start.2

commit v3 on v2

--- a/solution.py
+++ b/solution.py
@@ -27,6 +27,12 @@
 B_OWN = B_RL + RELAY
 B_ZERO = B_OWN + MAIN
 B_SIZE = B_ZERO + 1
+T_RELAY = RECEIVED
+T_GIVER = T_RELAY + 2 * RELAY
+T_PLACE = T_GIVER + RECEIVED
+T_RIGHT = T_PLACE + REFS
+T_LEFT = T_RIGHT + 1
+T_SIZE = T_LEFT + 1
 PIECES = 2
 DEEP = 8
 F32 = jnp.float32
@@ -72,20 +78,21 @@
     )
     relay_rank = jnp.where(right_way, rank, rank - by_right)
     code = jnp.where(away == 2, TARGETS + relay_rank, target)
-    spots = jnp.arange(RECEIVED, dtype=jnp.int32)
-    hit = place[..., None] == spots
-    merged = jnp.sum(jnp.where(hit, code[..., None], 0), axis=2)
     relay_place = jnp.where(away == 2, jnp.where(right_way, 0, RELAY) + relay_rank, -1)
-    relays = jnp.sum(
-        jnp.where(
-            relay_place[..., None] == jnp.arange(2 * RELAY, dtype=jnp.int32), target[..., None], 0
-        ),
-        axis=2,
-    )
-    own_place = lax.dynamic_slice_in_dim(place, x, 1, 1)[:, 0]
-    giver = jnp.sum(
-        jnp.where(own_place[..., None] == spots, entry[None, :, None], 0), axis=1
-    )
+    spots = jnp.arange(T_SIZE, dtype=jnp.int32)
+    where = [place, relay_place + T_RELAY, place + T_GIVER, entry + T_PLACE]
+    what = [code, target, entry, place]
+    where[1] = jnp.where(relay_place >= 0, where[1], -1)
+    lowest = (0, T_RELAY, T_GIVER, T_PLACE)
+    at, put = (jnp.broadcast_to(a[0], named.shape)[..., None] for a in (where, what))
+    for low, at_next, put_next in zip(lowest[1:], where[1:], what[1:]):
+        at = jnp.where(spots >= low, jnp.broadcast_to(at_next, named.shape)[..., None], at)
+        put = jnp.where(spots >= low, jnp.broadcast_to(put_next, named.shape)[..., None], put)
+    hit = at == spots
+    hit = jnp.where(spots == T_RIGHT, (away == 1)[..., None], hit)
+    hit = jnp.where(spots == T_LEFT, (away == 3)[..., None], hit)
+    put = jnp.where(spots >= T_RIGHT, 1, put)
+    first = jnp.sum(jnp.where(hit, put, 0), axis=2)
     landing = jnp.where(
         away == 0,
         B_OWN + rank,
@@ -106,52 +113,44 @@
     sources = B_ZERO + jnp.sum(
         jnp.where(cell[:, :, None] == cells, landing[:, :, None] - B_ZERO, 0), axis=1
     )
-    counts = jnp.stack((n_r, n_l), axis=-1).reshape(H, 2 * NX)
-    return (
-        merged.reshape(H, NX * RECEIVED),
-        relays.reshape(H, NX * 2 * RELAY),
-        own_place,
-        giver,
-        counts,
-        sources,
-    )
+    return first, sources
 
 
 ORDER = (
-    ("GS", 0), ("PO", 0), ("PO", 1), ("PO", 2), ("PO", 3), ("G", 0, 2, 0), ("G", 0, 2, 1),
-    ("G", 0, 3, 0), ("G", 0, 3, 1), ("GS", 1), ("G", 0, 4, 0), ("G", 0, 4, 1), ("G", 1, 2, 0),
-    ("G", 1, 2, 1), ("GE", 0), ("SR", 0), ("G", 1, 3, 0), ("G", 1, 3, 1), ("GS", 2),
-    ("G", 1, 4, 0), ("SM", 0), ("G", 1, 4, 1), ("G", 2, 2, 0), ("G", 2, 2, 1), ("GE", 1),
-    ("SR", 1), ("G", 2, 3, 0), ("G", 2, 3, 1), ("GS", 3), ("G", 2, 4, 0), ("SM", 1),
-    ("G", 2, 4, 1), ("G", 3, 2, 0), ("G", 3, 2, 1), ("GE", 2), ("SR", 2), ("G", 3, 3, 0),
-    ("G", 3, 3, 1), ("C", 0, 0), ("SM", 2), ("G", 3, 4, 0), ("G", 3, 4, 1), ("C", 0, 1), ("ST", 0),
-    ("GE", 3), ("SR", 3), ("ST", 1), ("GS", 4), ("G", 4, 2, 0), ("G", 4, 2, 1), ("G", 4, 3, 0),
-    ("G", 4, 3, 1), ("GS", 5), ("RT", 0), ("G", 4, 4, 0), ("G", 4, 4, 1), ("SM", 3),
-    ("G", 5, 2, 0), ("G", 5, 2, 1), ("GE", 4), ("SR", 4), ("G", 5, 3, 0), ("RT", 1),
-    ("G", 5, 3, 1), ("GS", 6), ("G", 5, 4, 0), ("L", 0), ("R", 0, 1), ("SS", 0), ("R", 0, 2),
-    ("G", 5, 4, 1), ("R", 0, 3), ("R", 0, 4), ("R", 0, 5), ("G", 6, 2, 0), ("G", 6, 2, 1),
-    ("S", 0, 2, 0), ("S", 0, 2, 1), ("C", 1, 0), ("SM", 4), ("G", 6, 3, 0), ("G", 6, 3, 1),
-    ("GE", 5), ("SR", 5), ("S", 0, 3, 0), ("C", 1, 1), ("S", 0, 3, 1), ("L", 1), ("ST", 2),
-    ("G", 6, 4, 0), ("G", 6, 4, 1), ("R", 1, 1), ("SS", 1), ("R", 1, 2), ("R", 1, 3),
-    ("S", 0, 4, 0), ("R", 1, 4), ("R", 1, 5), ("ST", 3), ("S", 0, 4, 1), ("GS", 7), ("GE", 6),
-    ("SR", 6), ("SM", 5), ("S", 1, 2, 0), ("S", 1, 2, 1), ("F", 0), ("G", 7, 2, 0), ("RT", 2),
-    ("G", 7, 2, 1), ("S", 1, 3, 0), ("S", 1, 3, 1), ("G", 7, 3, 0), ("RT", 3), ("G", 7, 3, 1),
-    ("S", 1, 4, 0), ("SM", 6), ("S", 1, 4, 1), ("G", 7, 4, 0), ("G", 7, 4, 1), ("C", 2, 0),
-    ("L", 2), ("F", 1), ("R", 2, 1), ("SS", 2), ("R", 2, 2), ("R", 2, 3), ("R", 2, 4), ("R", 2, 5),
-    ("GE", 7), ("SR", 7), ("L", 3), ("R", 3, 1), ("SS", 3), ("R", 3, 2), ("R", 3, 3),
-    ("S", 2, 2, 0), ("S", 2, 2, 1), ("R", 3, 4), ("R", 3, 5), ("C", 2, 1), ("S", 2, 3, 0),
-    ("S", 3, 2, 0), ("S", 2, 3, 1), ("S", 3, 2, 1), ("ST", 4), ("ST", 5), ("SM", 7),
-    ("S", 2, 4, 0), ("S", 3, 3, 0), ("S", 2, 4, 1), ("S", 3, 3, 1), ("RT", 4), ("S", 3, 4, 0),
-    ("F", 2), ("S", 3, 4, 1), ("RT", 5), ("F", 3), ("C", 3, 0), ("L", 4), ("R", 4, 1), ("SS", 4),
-    ("R", 4, 2), ("R", 4, 3), ("R", 4, 4), ("R", 4, 5), ("C", 3, 1), ("S", 4, 2, 0),
-    ("S", 4, 2, 1), ("L", 5), ("ST", 6), ("R", 5, 1), ("SS", 5), ("R", 5, 2), ("R", 5, 3),
-    ("R", 5, 4), ("R", 5, 5), ("ST", 7), ("S", 4, 3, 0), ("S", 4, 3, 1), ("S", 5, 2, 0),
-    ("S", 5, 2, 1), ("S", 4, 4, 0), ("RT", 6), ("S", 4, 4, 1), ("S", 5, 3, 0), ("S", 5, 3, 1),
-    ("RT", 7), ("F", 4), ("S", 5, 4, 0), ("L", 6), ("R", 6, 1), ("SS", 6), ("S", 5, 4, 1),
-    ("R", 6, 2), ("R", 6, 3), ("R", 6, 4), ("R", 6, 5), ("L", 7), ("R", 7, 1), ("SS", 7),
-    ("R", 7, 2), ("S", 6, 2, 0), ("S", 6, 2, 1), ("R", 7, 3), ("R", 7, 4), ("F", 5), ("R", 7, 5),
-    ("S", 7, 2, 0), ("S", 7, 2, 1), ("S", 6, 3, 0), ("S", 6, 3, 1), ("S", 7, 3, 0), ("S", 7, 3, 1),
-    ("S", 6, 4, 0), ("S", 6, 4, 1), ("S", 7, 4, 0), ("S", 7, 4, 1), ("F", 6), ("F", 7),
+    ("GS", 0), ("G", 0, 2, 0), ("G", 0, 2, 1), ("G", 0, 3, 0), ("G", 0, 3, 1), ("GS", 1),
+    ("G", 0, 4, 0), ("G", 0, 4, 1), ("G", 1, 2, 0), ("G", 1, 2, 1), ("GE", 0), ("SR", 0),
+    ("G", 1, 3, 0), ("G", 1, 3, 1), ("GS", 2), ("SM", 0), ("G", 1, 4, 0), ("G", 1, 4, 1),
+    ("G", 2, 2, 0), ("GE", 1), ("G", 2, 2, 1), ("SR", 1), ("G", 2, 3, 0), ("G", 2, 3, 1),
+    ("GS", 3), ("G", 2, 4, 0), ("SM", 1), ("G", 2, 4, 1), ("G", 3, 2, 0), ("GE", 2),
+    ("G", 3, 2, 1), ("SR", 2), ("G", 3, 3, 0), ("C", 0, 0), ("SM", 2), ("G", 3, 3, 1), ("GS", 4),
+    ("C", 0, 1), ("G", 3, 4, 0), ("G", 3, 4, 1), ("ST", 0), ("G", 4, 2, 0), ("G", 4, 2, 1),
+    ("ST", 1), ("G", 4, 3, 0), ("GE", 3), ("G", 4, 3, 1), ("GS", 5), ("SR", 3), ("G", 4, 4, 0),
+    ("RT", 0), ("G", 4, 4, 1), ("G", 5, 2, 0), ("G", 5, 2, 1), ("G", 5, 3, 0), ("GE", 4),
+    ("G", 5, 3, 1), ("GS", 6), ("RT", 1), ("G", 5, 4, 0), ("SM", 3), ("G", 5, 4, 1),
+    ("G", 6, 2, 0), ("SR", 4), ("L", 0), ("G", 6, 2, 1), ("R", 0, 2), ("GE", 5), ("SR", 5),
+    ("R", 0, 3), ("G", 6, 3, 0), ("R", 0, 1), ("SM", 4), ("L", 1), ("R", 1, 2), ("R", 1, 1),
+    ("G", 6, 3, 1), ("SS", 0), ("GS", 7), ("C", 1, 0), ("SM", 5), ("G", 6, 4, 0), ("G", 7, 2, 0),
+    ("C", 1, 1), ("SS", 1), ("S", 0, 2, 0), ("ST", 2), ("R", 1, 5), ("G", 6, 4, 1), ("R", 1, 3),
+    ("R", 0, 4), ("S", 1, 2, 0), ("ST", 3), ("C", 2, 0), ("G", 7, 2, 1), ("S", 0, 2, 1), ("RT", 2),
+    ("GE", 6), ("S", 1, 2, 1), ("G", 7, 3, 0), ("C", 2, 1), ("S", 0, 3, 0), ("R", 1, 4),
+    ("G", 7, 3, 1), ("RT", 3), ("ST", 5), ("L", 2), ("S", 1, 3, 0), ("R", 2, 2), ("S", 1, 3, 1),
+    ("G", 7, 4, 0), ("L", 3), ("G", 7, 4, 1), ("S", 1, 4, 0), ("R", 3, 1), ("S", 1, 4, 1),
+    ("R", 3, 5), ("S", 0, 3, 1), ("SS", 3), ("SR", 6), ("S", 0, 4, 0), ("R", 3, 3), ("R", 2, 1),
+    ("R", 3, 2), ("GE", 7), ("R", 2, 3), ("SR", 7), ("S", 0, 4, 1), ("F", 1), ("SM", 6),
+    ("S", 3, 2, 0), ("R", 2, 4), ("SS", 2), ("R", 3, 4), ("S", 3, 2, 1), ("R", 0, 5),
+    ("S", 3, 3, 0), ("SM", 7), ("ST", 4), ("F", 0), ("S", 2, 2, 0), ("RT", 5), ("S", 2, 2, 1),
+    ("S", 2, 3, 0), ("S", 3, 3, 1), ("R", 2, 5), ("S", 2, 3, 1), ("S", 2, 4, 0), ("C", 3, 0),
+    ("S", 3, 4, 0), ("S", 2, 4, 1), ("S", 3, 4, 1), ("RT", 4), ("C", 3, 1), ("L", 5), ("R", 5, 1),
+    ("SS", 5), ("ST", 6), ("R", 5, 2), ("ST", 7), ("L", 4), ("R", 4, 1), ("SS", 4), ("R", 4, 2),
+    ("F", 3), ("S", 5, 2, 0), ("R", 4, 3), ("S", 5, 2, 1), ("R", 4, 4), ("F", 2), ("S", 4, 2, 0),
+    ("R", 5, 5), ("S", 4, 2, 1), ("R", 5, 3), ("S", 5, 3, 0), ("S", 4, 3, 0), ("R", 5, 4),
+    ("R", 4, 5), ("S", 4, 3, 1), ("S", 5, 3, 1), ("RT", 6), ("RT", 7), ("S", 4, 4, 0),
+    ("S", 5, 4, 0), ("L", 6), ("S", 4, 4, 1), ("R", 6, 2), ("R", 6, 1), ("SS", 6), ("S", 5, 4, 1),
+    ("L", 7), ("R", 7, 3), ("R", 7, 1), ("R", 7, 2), ("SS", 7), ("F", 4), ("S", 6, 2, 0),
+    ("S", 6, 2, 1), ("F", 5), ("R", 6, 3), ("S", 7, 2, 0), ("R", 6, 5), ("S", 7, 2, 1),
+    ("R", 6, 4), ("S", 6, 3, 0), ("R", 7, 4), ("S", 7, 3, 0), ("S", 7, 3, 1), ("S", 6, 3, 1),
+    ("R", 7, 5), ("S", 7, 4, 0), ("S", 6, 4, 0), ("S", 6, 4, 1), ("S", 7, 4, 1), ("F", 6),
+    ("F", 7),
 )
 
 
@@ -159,11 +158,7 @@
     kv,
     query,
     grad,
-    merged_t,
-    relay_t,
-    place_t,
-    giver_t,
-    count_t,
+    slot_t,
     source_t,
     out_o,
     out_q,
@@ -190,7 +185,9 @@
     anchor_kv,
     wide,
     terms,
+    ag_sent,
     ag_sem,
+    rs_sent,
     rs_sem,
     x_sem,
     anchor_sem,
@@ -211,36 +208,47 @@
     rim = (z == 0) | (z == NZ - 1)
     beyond = lax.rem(jnp.where(z == 0, ctx + NX * NZ - 1, ctx + 1), NX * NZ)
 
-    def to(device, src, dst, sems):
+    def to(device, src, dst, sent, came=None):
         return pltpu.make_async_remote_copy(
             src_ref=src,
             dst_ref=dst,
-            send_sem=sems.at[0],
-            recv_sem=sems.at[1],
+            send_sem=sent if came is not None else sent.at[0],
+            recv_sem=came if came is not None else sent.at[1],
             device_id={"ctx": device},
             device_id_type=MESH,
         )
 
     barrier = pltpu.get_barrier_semaphore()
 
+    def place_own(u):
+        @pl.loop(0, BPD)
+        def _(b):
+            table[u][z * BPD + b] = kv[u, b]
+
     def greet(device):
         pl.semaphore_signal(barrier, inc=1, device_id={"ctx": device}, device_id_type=MESH)
 
     for device in (z_r, z_l, x_r, x_l):
         greet(device)
 
+    for u in range(UNITS):
+        place_own(u)
+
     @pl.when(rim)
     def _():
-        greet(beyond)
-
-    pl.semaphore_wait(barrier, 4 + rim.astype(jnp.int32))
+        @pl.loop(0, UNITS)
+        def _(u):
+            edge_out[u] = kv[u, jnp.where(z == 0, 0, BPD - 1)]
+
+    pl.semaphore_wait(barrier, 4)
 
     def gather_copy(u, s, half, right):
         row = lax.rem(z + NZ - (s - 1), NZ) if right else lax.rem(z + s - 1, NZ)
         cut = pl.ds(row * BPD + half * HALF, HALF)
         src = kv.at[u, pl.ds(half * HALF, HALF)] if s == 1 else table[u].at[cut]
         way = 0 if right else 1
-        return to(z_r if right else z_l, src, table[u].at[cut], ag_sem.at[u, s - 1, half, way])
+        came = ag_sem.at[u % 2, s - 1, half, way]
+        return to(z_r if right else z_l, src, table[u].at[cut], ag_sent.at[u], came)
 
     def moves(s):
         return [
@@ -264,17 +272,12 @@
         for half, right in moves(4):
             gather_copy(u, 4, half, right).wait_recv()
 
+    def all_sent(u, sent):
+        whole = table[u].at[pl.ds(0, 14 * HALF)]
+        to(z_r, whole, whole, sent.at[u], ag_sem.at[0, 0, 0, 0]).wait_send()
+
     def gather_sent(u):
-        for s in (1, 2, 3, 4):
-            for half, right in moves(s):
-                gather_copy(u, s, half, right).wait_send()
-
-    def place_own(h):
-        for p in (0, 1):
-
-            @pl.loop(0, BPD)
-            def _(b):
-                table[2 * h + p][z * BPD + b] = kv[2 * h + p, b]
+        all_sent(u, ag_sent)
 
     def edge_copy():
         return to(beyond, edge_out, edge_in, edge_sem.at[UNITS])
@@ -282,10 +285,6 @@
     def send_edges():
         @pl.when(rim)
         def _():
-            @pl.loop(0, UNITS)
-            def _(u):
-                edge_out[u] = kv[u, jnp.where(z == 0, 0, BPD - 1)]
-
             edge_copy().start()
 
     def relay_copy(u, side):
@@ -333,15 +332,15 @@
 
         @pl.loop(0, RELAY)
         def _(k):
-            relay_out[u][0, k] = table[u][relay_t[h, p_o * 2 * RELAY + RELAY + k]]
-            relay_out[u][1, k] = table[u][relay_t[h, p_o * 2 * RELAY + k]]
+            relay_out[u][0, k] = table[u][slot_t[h, p_o, T_RELAY + RELAY + k]]
+            relay_out[u][1, k] = table[u][slot_t[h, p_o, T_RELAY + k]]
 
         for side in (0, 1):
             relay_copy(u, side).start()
 
         @pl.loop(0, MAIN)
         def _(k):
-            received[u][OWN + k] = table[u][merged_t[h, x * RECEIVED + OWN + k]]
+            received[u][OWN + k] = table[u][slot_t[h, x, OWN + k]]
 
     def send_merged(u):
         h = u // 2
@@ -351,7 +350,7 @@
         @pl.loop(0, MAIN)
         def _(k):
             for side, plane, first, back in ((0, p_r, FROM_L, 1), (1, p_l, FROM_R, 0)):
-                code = merged_t[h, plane * RECEIVED + first + k]
+                code = slot_t[h, plane, first + k]
                 direct = table[u][jnp.minimum(code, TARGETS - 1)]
                 passed = relay_in[u][back, jnp.maximum(code - TARGETS, 0)]
                 merged_out[u][side, k] = jnp.where(code < TARGETS, direct, passed)
@@ -363,6 +362,9 @@
         @pl.when(inner)
         def _():
             anchor_pass(u).start()
+
+        if u == 0:
+            send_edges()
 
     def lay_keys(h):
         for p in (0, 1):
@@ -402,7 +404,7 @@
         @pl.loop(piece * BPD // PIECES, (piece + 1) * BPD // PIECES)
         def _(i):
             rows = pl.ds(pl.multiple_of(i * BLOCK, BLOCK), 3 * BLOCK)
-            spots = [place_t[h, i * R + r] for r in range(R)]
+            spots = [slot_t[h, x, T_PLACE + i * R + r] for r in range(R)]
             keys, values = (
                 jnp.concatenate(
                     [wide[p, rows], anchor_kv[p]] + [received[2 * h + p][s] for s in spots], axis=0
@@ -484,9 +486,9 @@
 
         @pl.loop(0, MAIN)
         def _(k):
-            merged_out[u][0, k] = terms[p, giver_t[h, FROM_R + k]]
-            merged_out[u][1, k] = terms[p, giver_t[h, FROM_L + k]]
-            terms_in[u][B_OWN + k] = terms[p, giver_t[h, OWN + k]]
+            merged_out[u][0, k] = terms[p, slot_t[h, x, T_GIVER + FROM_R + k]]
+            merged_out[u][1, k] = terms[p, slot_t[h, x, T_GIVER + FROM_L + k]]
+            terms_in[u][B_OWN + k] = terms[p, slot_t[h, x, T_GIVER + OWN + k]]
 
         for side in (0, 1):
             terms_copy(u, side).start()
@@ -510,8 +512,8 @@
 
         @pl.loop(0, RELAY)
         def _(k):
-            from_left = count_t[h, p_l * 2] + k
-            from_right = count_t[h, p_r * 2 + 1] + k
+            from_left = slot_t[h, p_l, T_RIGHT] + k
+            from_right = slot_t[h, p_r, T_LEFT] + k
             relay_out[u][0, k] = terms_in[u][FROM_L + jnp.minimum(from_left, MAIN - 1)]
             relay_out[u][1, k] = terms_in[u][FROM_R + jnp.minimum(from_right, MAIN - 1)]
 
@@ -599,7 +601,8 @@
             z_r if right else z_l,
             table[u].at[pl.ds(row * BPD + half * HALF, HALF)],
             (sums_r if right else sums_l)[u].at[s - 1, pl.ds(half * HALF, HALF)],
-            rs_sem.at[u, s - 1, half, way],
+            rs_sent.at[u],
+            rs_sem.at[u % 2, s - 1, half, way],
         )
 
     def sum_moves(s):
@@ -647,9 +650,7 @@
             (out_k, out_v)[p][h, b] = total.astype(BF16)
 
     def drain(u):
-        for s in (1, 2, 3, 4):
-            for half, right in sum_moves(s):
-                sum_copy(u, s, half, right).wait_send()
+        all_sent(u, rs_sent)
         for side in (0, 1):
             terms_copy(u, side).wait_send()
             terms_relay_copy(u, side).wait_send()
@@ -675,7 +676,6 @@
         "GS": gather_start,
         "G": gather_step,
         "GE": gather_end,
-        "PO": place_own,
         "SR": send_relays,
         "SM": send_merged,
         "C": compute,
@@ -687,7 +687,6 @@
         "S": sum_step,
         "F": finish,
     }
-    send_edges()
     for name, *where in ORDER:
         steps[name](*where)
     for u in range(UNITS):
@@ -742,8 +741,10 @@
             pltpu.VMEM((2, 2 * BLOCK, HD), BF16),
             pltpu.VMEM((2, (BPD + 2) * BLOCK, HD), BF16),
             pltpu.VMEM((2, REFS, *block), BF16),
-            dma((UNITS, 4, 2, 2, 2)),
-            dma((UNITS, 4, 2, 2, 2)),
+            dma((UNITS,)),
+            dma((2, 4, 2, 2)),
+            dma((UNITS,)),
+            dma((2, 4, 2, 2)),
             dma((4, UNITS, 2, 2)),
             dma((UNITS, 3, 2)),
             dma((UNITS, 3, 2)),

time: 229 us -> 222 us (0.969)
  Pallas kernels: 210 us -> 206 us
  local copies, waits for them, and re-layouts: 12.8 us -> 10.3 us
    pallas_call x1, Pallas kernels: 210 us -> 206 us  [local(): pl.pallas_call(kernel, out_shape=[jax.ShapeDtypeStruct((H, BPD, BLOCK, HD...]
    unnamed x23 -> x20, local copies, waits for them, and re-layouts: 8.52 us -> 8.51 us
where the time goes in v3:
time: 222 us
  Pallas kernels  206 us (93%)
  local copies, waits for them, and re-layouts  10.3 us (5%)
  other arithmetic  4.98 us (2%)
    pallas_call x1, Pallas kernels, local(): pl.pallas_call(kernel, out_shape=[jax.ShapeDtypeStruct((H, BPD, BLOCK, HD...  206 us
    unnamed x20, local copies, waits for them, and re-layouts  8.51 us

profile of v3, /device:TPU:16, one launch (start us, length us, event | category | flops | bytes accessed | tf_op | source)
XLA Modules:
  0.0 221.8 jit_solution(12148374768954348277)
XLA Ops:
  0.6 0.0 copy-start
  0.7 0.1 sub.126
  0.8 0.8 reshape.494
  1.7 0.2 copy.30
  1.9 0.1 reshape.496
  2.0 1.0 convert_reduce_fusion.2
  3.0 0.1 reshape.495
  3.1 0.1 lt.96
  3.1 0.1 lt.104
  3.3 0.5 convert_reduce_fusion.1
  3.7 0.1 reduce_sum.71
  3.8 0.2 convert_reduce_fusion
  4.1 0.2 select_reduce_fusion
  4.3 0.6 broadcast_add_fusion.source_t
  4.9 0.1 broadcast_add_fusion.1
  5.0 0.1 add_select_fusion.2
  5.1 1.2 select_reduce_fusion.1.slot_t
  6.2 0.0 copy-done
  6.2 0.0 copy-start.1
  6.2 0.9 copy.28
  7.1 0.3 copy-done.1
  7.4 0.0 copy-start.5
  7.4 0.0 copy-start.6
  7.4 0.9 copy.29
  8.3 0.3 copy-done.5
  8.6 0.2 copy-done.6
  8.8 0.2 copy_bitcast_fusion
  9.1 1.1 pad_maximum_fusion
  10.2 205.7 %shard_map.84 = (bf16[4,8,64,128]{3,2,1,0:T(8,128)(2,1)}, bf16[4,8,64,128]{3,2,1,0:T(8,128)(2,1)}, bf16[4,8,64,128]{3,2,1,0:T(8,128)(2,1)}, bf16[4,8,64,128]{3,2,1,0:T(8,128)(2,1)}) custom-call(bf16[8,8,64,128]{3,2,1,0:T(8,128)(2,1)} %bitcast.39, bf16[4,8,64,128]{3,2,1,0:T(8,128)(2,1)} %bitcast.42, bf16[4,8,64,128]{3,2,1,0:T(8,128)(2,1)} %bitcast.43, ...), custom_call_target="tpu_custom_call" | custom-call | flops 1610612736 | bytes 4194304 | tf_op jit(solution)/shard_map/pallas_call | solution.py:717
  215.8 0.0 copy-start.4
  215.8 2.3 %copy.31 = bf16[512,4,128]{2,1,0:T(4,128)(2,1)} copy(bf16[512,4,128]{2,0,1:T(8,128)(2,1)} %bitcast.47) | data formatting | bytes 1048576
  218.1 0.0 copy-done.4
  218.1 0.0 copy-start.3
  218.1 1.2 copy.32
  219.3 0.0 copy-done.3
  219.4 0.0 copy-start.2
  219.4 1.2 copy.33
  220.6 0.0 copy-done.2
  220.6 1.2 copy.34
  (13 shorter events, 0.1 us)
Async XLA Ops:
  0.6 5.6 %copy-start = (bf16[512,4,128]{2,1,0:T(4,128)(2,1)S(1)}, bf16[512,4,128]{2,1,0:T(4,128)(2,1)}, u32[]{:S(2)}) copy-start(bf16[512,4,128]{2,1,0:T(4,128)(2,1)} %param.5) | copy-start | bytes 1572868
  6.2 1.2 copy-start.1
  7.4 1.2 copy-start.5
  7.4 1.4 copy-start.6
  215.8 2.3 %copy-start.4 = (bf16[4,8,64,128]{3,2,1,0:T(8,128)(2,1)S(1)}, bf16[4,8,64,128]{3,2,1,0:T(8,128)(2,1)}, u32[]{:S(2)}) copy-start(bf16[4,8,64,128]{3,2,1,0:T(8,128)(2,1)} %get-tuple-element.9) | copy-start | bytes 1572868
  218.1 1.2 copy-start.3
  219.4 1.2 copy-start.2

commit v4 on v3

--- a/solution.py
+++ b/solution.py
@@ -32,7 +32,7 @@
 T_PLACE = T_GIVER + RECEIVED
 T_RIGHT = T_PLACE + REFS
 T_LEFT = T_RIGHT + 1
-T_SIZE = T_LEFT + 1
+T_WIDTH = 256
 PIECES = 2
 DEEP = 8
 F32 = jnp.float32
@@ -41,58 +41,73 @@
 SCALE = 1.0 / math.sqrt(HD)
 
 
-def slot_tables(links):
-    ctx = lax.axis_index("ctx")
-    x, z = ctx // NZ, ctx % NZ
+def named_blocks(links):
+    z = lax.axis_index("ctx") % NZ
     row = lax.dynamic_slice_in_dim(links.reshape(NX, NZ, BPD, H, R), z, 1, 1)[:, 0]
-    named = row.transpose(2, 0, 1, 3).reshape(H, NX, REFS)
-    planes = jnp.arange(NX, dtype=jnp.int32)
-    away = (named // TARGETS - planes[None, :, None]) % NX
-    target = named % TARGETS
-    entry = jnp.arange(REFS, dtype=jnp.int32)
-    before = entry[None, :] < entry[:, None]
-    rank = jnp.sum(
-        ((away[..., None, :] == away[..., :, None]) & before).astype(jnp.int32), axis=-1
-    )
-    n_r = jnp.sum((away == 1).astype(jnp.int32), axis=-1)
-    n_o = jnp.sum((away == 2).astype(jnp.int32), axis=-1)
-    n_l = jnp.sum((away == 3).astype(jnp.int32), axis=-1)
-    by_right = jnp.minimum(n_o, jnp.minimum(RELAY, MAIN - n_r))[..., None]
+    return row.transpose(0, 2, 1, 3).reshape(NX * H, REFS)
+
+
+def slot_tables(named, x):
+    plane = lax.broadcasted_iota(jnp.int32, named.shape, 0) // H
+    lane = lax.broadcasted_iota(jnp.int32, named.shape, 1)
+    away = ((named >> 6) - plane) & (NX - 1)
+    target = named & (TARGETS - 1)
+
+    def entry(array, e):
+        return array[:, e : e + 1]
+
+    rank = jnp.zeros_like(named)
+    n_r, n_o, n_l = (jnp.zeros((NX * H, 1), jnp.int32) for _ in range(3))
+    for e in range(REFS):
+        way = entry(away, e)
+        rank += jnp.where((away == way) & (lane > e), 1, 0)
+        n_r += jnp.where(way == 1, 1, 0)
+        n_o += jnp.where(way == 2, 1, 0)
+        n_l += jnp.where(way == 3, 1, 0)
+    by_right = jnp.minimum(n_o, jnp.minimum(RELAY, MAIN - n_r))
     right_way = rank < by_right
+    relay_rank = jnp.where(right_way, rank, rank - by_right)
+    opposite = jnp.where(right_way, FROM_R + n_r + rank, FROM_L + n_l + relay_rank)
     place = jnp.where(
         away == 0,
         OWN + rank,
+        jnp.where(away == 1, FROM_R + rank, jnp.where(away == 3, FROM_L + rank, opposite)),
+    )
+    code = jnp.where(away == 2, TARGETS + relay_rank, target)
+    relay_place = jnp.where(
+        away == 2, T_RELAY + relay_rank + jnp.where(right_way, 0, RELAY), -1
+    )
+    spots = lax.broadcasted_iota(jnp.int32, (NX * H, T_WIDTH), 1)
+    first = jnp.where(spots == T_RIGHT, n_r, jnp.where(spots == T_LEFT, n_l, 0))
+    for e in range(REFS):
+        here = entry(place, e)
+        at = jnp.where(
+            spots < T_RELAY,
+            here,
+            jnp.where(
+                spots < T_GIVER,
+                entry(relay_place, e),
+                jnp.where(spots < T_PLACE, T_GIVER + here, T_PLACE + e),
+            ),
+        )
+        put = jnp.where(
+            spots < T_RELAY,
+            entry(code, e),
+            jnp.where(
+                spots < T_GIVER, entry(target, e), jnp.where(spots < T_PLACE, e, here)
+            ),
+        )
+        first += jnp.where(at == spots, put, 0)
+    most = jnp.where(
+        spots < T_RELAY,
+        TARGETS + RELAY - 1,
         jnp.where(
-            away == 1,
-            FROM_R + rank,
-            jnp.where(
-                away == 3,
-                FROM_L + rank,
-                jnp.where(
-                    right_way,
-                    FROM_R + n_r[..., None] + rank,
-                    FROM_L + n_l[..., None] + rank - by_right,
-                ),
-            ),
+            spots < T_GIVER,
+            TARGETS - 1,
+            jnp.where(spots < T_PLACE, REFS - 1, jnp.where(spots < T_RIGHT, RECEIVED - 1, REFS)),
         ),
     )
-    relay_rank = jnp.where(right_way, rank, rank - by_right)
-    code = jnp.where(away == 2, TARGETS + relay_rank, target)
-    relay_place = jnp.where(away == 2, jnp.where(right_way, 0, RELAY) + relay_rank, -1)
-    spots = jnp.arange(T_SIZE, dtype=jnp.int32)
-    where = [place, relay_place + T_RELAY, place + T_GIVER, entry + T_PLACE]
-    what = [code, target, entry, place]
-    where[1] = jnp.where(relay_place >= 0, where[1], -1)
-    lowest = (0, T_RELAY, T_GIVER, T_PLACE)
-    at, put = (jnp.broadcast_to(a[0], named.shape)[..., None] for a in (where, what))
-    for low, at_next, put_next in zip(lowest[1:], where[1:], what[1:]):
-        at = jnp.where(spots >= low, jnp.broadcast_to(at_next, named.shape)[..., None], at)
-        put = jnp.where(spots >= low, jnp.broadcast_to(put_next, named.shape)[..., None], put)
-    hit = at == spots
-    hit = jnp.where(spots == T_RIGHT, (away == 1)[..., None], hit)
-    hit = jnp.where(spots == T_LEFT, (away == 3)[..., None], hit)
-    put = jnp.where(spots >= T_RIGHT, 1, put)
-    first = jnp.sum(jnp.where(hit, put, 0), axis=2)
+    first = jnp.clip(first, 0, most)
     landing = jnp.where(
         away == 0,
         B_OWN + rank,
@@ -103,17 +118,25 @@
                 away == 3, FROM_R + rank, jnp.where(right_way, B_RL, B_RR) + relay_rank
             ),
         ),
-    ).reshape(H, NX * REFS)
-    here = jnp.where(named // TARGETS == x, target, -1).reshape(H, NX * REFS)
-    every = jnp.arange(NX * REFS, dtype=jnp.int32)
-    same = (here[:, None, :] == here[:, :, None]) & (every[None, :] < every[:, None])
-    depth = jnp.sum(same.astype(jnp.int32), axis=-1)
-    cell = jnp.where(here >= 0, here * DEEP + depth, -1)
-    cells = jnp.arange(TARGETS * DEEP, dtype=jnp.int32)
-    sources = B_ZERO + jnp.sum(
-        jnp.where(cell[:, :, None] == cells, landing[:, :, None] - B_ZERO, 0), axis=1
     )
-    return first, sources
+    mine = jnp.where((named >> 6) == x, target, -1)
+    cells = lax.broadcasted_iota(jnp.int32, (H, TARGETS * DEEP), 1)
+    sources = jnp.full((H, TARGETS * DEEP), B_ZERO, jnp.int32)
+    parts = [slice(a * H, (a + 1) * H) for a in range(NX)]
+    for a in range(NX):
+        aim = mine[parts[a]]
+        depth = jnp.zeros_like(aim)
+        for b in range(a + 1):
+            for e in range(REFS):
+                same = aim == entry(mine[parts[b]], e)
+                if b == a:
+                    same = same & (lane[:H] > e)
+                depth += jnp.where(same, 1, 0)
+        cell = jnp.where(aim >= 0, aim * DEEP + depth, -1)
+        land = landing[parts[a]]
+        for e in range(REFS):
+            sources += jnp.where(entry(cell, e) == cells, entry(land, e) - B_ZERO, 0)
+    return first, jnp.clip(sources, 0, B_SIZE - 1)
 
 
 ORDER = (
@@ -158,8 +181,7 @@
     kv,
     query,
     grad,
-    slot_t,
-    source_t,
+    links,
     out_o,
     out_q,
     out_k,
@@ -193,6 +215,11 @@
     anchor_sem,
     part_sem,
     edge_sem,
+    slot_v,
+    source_v,
+    slot_t,
+    source_t,
+    table_sem,
 ):
     ctx = lax.axis_index("ctx")
     x, z = ctx // NZ, ctx % NZ
@@ -231,6 +258,13 @@
     for device in (z_r, z_l, x_r, x_l):
         greet(device)
 
+    slot_v[...], source_v[...] = slot_tables(links[...], x)
+    copies = (
+        pltpu.make_async_copy(slot_v, slot_t, table_sem.at[0]),
+        pltpu.make_async_copy(source_v, source_t, table_sem.at[1]),
+    )
+    for copy in copies:
+        copy.start()
     for u in range(UNITS):
         place_own(u)
 
@@ -240,6 +274,8 @@
         def _(u):
             edge_out[u] = kv[u, jnp.where(z == 0, 0, BPD - 1)]
 
+    for copy in copies:
+        copy.wait()
     pl.semaphore_wait(barrier, 4)
 
     def gather_copy(u, s, half, right):
@@ -332,15 +368,15 @@
 
         @pl.loop(0, RELAY)
         def _(k):
-            relay_out[u][0, k] = table[u][slot_t[h, p_o, T_RELAY + RELAY + k]]
-            relay_out[u][1, k] = table[u][slot_t[h, p_o, T_RELAY + k]]
+            relay_out[u][0, k] = table[u][slot_t[p_o * H + h, T_RELAY + RELAY + k]]
+            relay_out[u][1, k] = table[u][slot_t[p_o * H + h, T_RELAY + k]]
 
         for side in (0, 1):
             relay_copy(u, side).start()
 
         @pl.loop(0, MAIN)
         def _(k):
-            received[u][OWN + k] = table[u][slot_t[h, x, OWN + k]]
+            received[u][OWN + k] = table[u][slot_t[x * H + h, OWN + k]]
 
     def send_merged(u):
         h = u // 2
@@ -350,7 +386,7 @@
         @pl.loop(0, MAIN)
         def _(k):
             for side, plane, first, back in ((0, p_r, FROM_L, 1), (1, p_l, FROM_R, 0)):
-                code = slot_t[h, plane, first + k]
+                code = slot_t[plane * H + h, first + k]
                 direct = table[u][jnp.minimum(code, TARGETS - 1)]
                 passed = relay_in[u][back, jnp.maximum(code - TARGETS, 0)]
                 merged_out[u][side, k] = jnp.where(code < TARGETS, direct, passed)
@@ -404,7 +440,7 @@
         @pl.loop(piece * BPD // PIECES, (piece + 1) * BPD // PIECES)
         def _(i):
             rows = pl.ds(pl.multiple_of(i * BLOCK, BLOCK), 3 * BLOCK)
-            spots = [slot_t[h, x, T_PLACE + i * R + r] for r in range(R)]
+            spots = [slot_t[x * H + h, T_PLACE + i * R + r] for r in range(R)]
             keys, values = (
                 jnp.concatenate(
                     [wide[p, rows], anchor_kv[p]] + [received[2 * h + p][s] for s in spots], axis=0
@@ -486,9 +522,9 @@
 
         @pl.loop(0, MAIN)
         def _(k):
-            merged_out[u][0, k] = terms[p, slot_t[h, x, T_GIVER + FROM_R + k]]
-            merged_out[u][1, k] = terms[p, slot_t[h, x, T_GIVER + FROM_L + k]]
-            terms_in[u][B_OWN + k] = terms[p, slot_t[h, x, T_GIVER + OWN + k]]
+            merged_out[u][0, k] = terms[p, slot_t[x * H + h, T_GIVER + FROM_R + k]]
+            merged_out[u][1, k] = terms[p, slot_t[x * H + h, T_GIVER + FROM_L + k]]
+            terms_in[u][B_OWN + k] = terms[p, slot_t[x * H + h, T_GIVER + OWN + k]]
 
         for side in (0, 1):
             terms_copy(u, side).start()
@@ -512,8 +548,8 @@
 
         @pl.loop(0, RELAY)
         def _(k):
-            from_left = slot_t[h, p_l, T_RIGHT] + k
-            from_right = slot_t[h, p_r, T_LEFT] + k
+            from_left = slot_t[p_l * H + h, T_RIGHT] + k
+            from_right = slot_t[p_r * H + h, T_LEFT] + k
             relay_out[u][0, k] = terms_in[u][FROM_L + jnp.minimum(from_left, MAIN - 1)]
             relay_out[u][1, k] = terms_in[u][FROM_R + jnp.minimum(from_right, MAIN - 1)]
 
@@ -704,7 +740,6 @@
     def seq_major(array):
         return array.transpose(1, 2, 0, 3).reshape(BPD * BLOCK, H, HD)
 
-    tables = slot_tables(random_links)
     kv = jnp.stack((head_major(key), head_major(value)), axis=1).reshape(UNITS, BPD, BLOCK, HD)
     block = (BLOCK, HD)
 
@@ -713,11 +748,10 @@
 
     dma = pltpu.SemaphoreType.DMA
     vmem = pl.BlockSpec(memory_space=pltpu.VMEM)
-    smem = pl.BlockSpec(memory_space=pltpu.SMEM)
     outs = pl.pallas_call(
         kernel,
         out_shape=[jax.ShapeDtypeStruct((H, BPD, BLOCK, HD), BF16)] * 4,
-        in_specs=[vmem] * 3 + [smem] * len(tables),
+        in_specs=[vmem] * 4,
         out_specs=[vmem] * 4,
         scratch_shapes=[
             per(UNITS, TARGETS, *block),
@@ -749,6 +783,11 @@
             dma((UNITS, 3, 2)),
             dma((UNITS, 3, 2)),
             dma((UNITS + 1, 2)),
+            pltpu.VMEM((NX * H, T_WIDTH), jnp.int32),
+            pltpu.VMEM((H, TARGETS * DEEP), jnp.int32),
+            pltpu.SMEM((NX * H, T_WIDTH), jnp.int32),
+            pltpu.SMEM((H, TARGETS * DEEP), jnp.int32),
+            dma((2,)),
         ],
         compiler_params=pltpu.CompilerParams(
             collective_id=0, has_side_effects=True, vmem_limit_bytes=60 * 2**20
@@ -758,7 +797,7 @@
             bytes_accessed=4 * 2**20,
             transcendentals=H * BPD * BLOCK * 8 * BLOCK,
         ),
-    )(kv, head_major(query), head_major(out_grad), *tables)
+    )(kv, head_major(query), head_major(out_grad), named_blocks(random_links))
     return tuple(seq_major(array) for array in outs)
 
 

time: 222 us -> 220 us (level)
  other arithmetic: 4.98 us -> 1.07 us
    reduce_sum x5 -> x0, other arithmetic: 3.01 us -> none  [the longest x1 1.15 us: slot_tables(): first = jnp.sum(jnp.where(hit, put, 0), axis=2)]
where the time goes in v4:
time: 220 us
  Pallas kernels  207 us (94%)
  local copies, waits for them, and re-layouts  11.3 us (5%)
    pallas_call x1, Pallas kernels, local(): pl.pallas_call(kernel, out_shape=[jax.ShapeDtypeStruct((H, BPD, BLOCK, HD...  207 us
    unnamed x20, local copies, waits for them, and re-layouts  9.95 us

profile of v4, /device:TPU:16, one launch (start us, length us, event | category | flops | bytes accessed | tf_op | source)
XLA Modules:
  0.0 219.9 jit_solution(16112908561686307164)
XLA Ops:
  0.6 0.0 copy-start.6
  0.7 0.7 copy-done.6
  1.3 0.1 reshape.46
  1.5 0.2 copy.22
  1.7 0.1 reshape.47
  1.8 0.7 copy.23.links
  2.4 0.0 copy-start
  2.4 2.0 copy.20
  4.4 0.0 copy-done
  4.4 0.0 copy-start.4
  4.4 0.0 copy-start.5
  4.4 0.9 copy.21
  5.3 0.3 copy-done.4
  5.6 0.2 copy-done.5
  5.8 0.2 copy_bitcast_fusion
  6.0 1.1 pad_maximum_fusion
  7.1 206.9 %shard_map.84 = (bf16[4,8,64,128]{3,2,1,0:T(8,128)(2,1)}, bf16[4,8,64,128]{3,2,1,0:T(8,128)(2,1)}, bf16[4,8,64,128]{3,2,1,0:T(8,128)(2,1)}, bf16[4,8,64,128]{3,2,1,0:T(8,128)(2,1)}) custom-call(bf16[8,8,64,128]{3,2,1,0:T(8,128)(2,1)} %bitcast.36, bf16[4,8,64,128]{3,2,1,0:T(8,128)(2,1)} %bitcast.37, bf16[4,8,64,128]{3,2,1,0:T(8,128)(2,1)} %bitcast.38, ...), custom_call_target="tpu_custom_call" | custom-call | flops 1610612736 | bytes 4194304 | tf_op jit(solution)/shard_map/pallas_call | solution.py:751
  214.0 0.0 copy-start.3
  214.0 2.3 %copy.24 = bf16[512,4,128]{2,1,0:T(4,128)(2,1)} copy(bf16[512,4,128]{2,0,1:T(8,128)(2,1)} %bitcast.42) | data formatting | bytes 1048576
  216.3 0.0 copy-done.3
  216.3 0.0 copy-start.2
  216.3 1.2 copy.25
  217.5 0.0 copy-done.2
  217.5 0.0 copy-start.1
  217.5 1.2 copy.26
  218.7 0.0 copy-done.1
  218.7 1.2 copy.27
  (1 shorter events, 0.0 us)
Async XLA Ops:
  0.6 0.7 copy-start.6
  2.4 2.0 copy-start
  4.4 1.2 copy-start.4
  4.4 1.4 copy-start.5
  214.0 2.3 %copy-start.3 = (bf16[4,8,64,128]{3,2,1,0:T(8,128)(2,1)S(1)}, bf16[4,8,64,128]{3,2,1,0:T(8,128)(2,1)}, u32[]{:S(2)}) copy-start(bf16[4,8,64,128]{3,2,1,0:T(8,128)(2,1)} %get-tuple-element.9) | copy-start | bytes 1572868
  216.3 1.2 copy-start.2
  217.5 1.2 copy-start.1

commit v5 on v4

--- a/solution.py
+++ b/solution.py
@@ -258,13 +258,6 @@
     for device in (z_r, z_l, x_r, x_l):
         greet(device)
 
-    slot_v[...], source_v[...] = slot_tables(links[...], x)
-    copies = (
-        pltpu.make_async_copy(slot_v, slot_t, table_sem.at[0]),
-        pltpu.make_async_copy(source_v, source_t, table_sem.at[1]),
-    )
-    for copy in copies:
-        copy.start()
     for u in range(UNITS):
         place_own(u)
 
@@ -274,8 +267,6 @@
         def _(u):
             edge_out[u] = kv[u, jnp.where(z == 0, 0, BPD - 1)]
 
-    for copy in copies:
-        copy.wait()
     pl.semaphore_wait(barrier, 4)
 
     def gather_copy(u, s, half, right):
@@ -723,7 +714,18 @@
         "S": sum_step,
         "F": finish,
     }
-    for name, *where in ORDER:
+    first_name, *first_where = ORDER[0]
+    steps[first_name](*first_where)
+    slot_v[...], source_v[...] = slot_tables(links[...], x)
+    copies = (
+        pltpu.make_async_copy(slot_v, slot_t, table_sem.at[0]),
+        pltpu.make_async_copy(source_v, source_t, table_sem.at[1]),
+    )
+    for copy in copies:
+        copy.start()
+    for copy in copies:
+        copy.wait()
+    for name, *where in ORDER[1:]:
         steps[name](*where)
     for u in range(UNITS):
         drain(u)

time: 220 us -> 219 us (level)
  no operation moved by 1% of the time
where the time goes in v5:
time: 219 us
  Pallas kernels  206 us (94%)
  local copies, waits for them, and re-layouts  11.3 us (5%)
    pallas_call x1, Pallas kernels, local(): pl.pallas_call(kernel, out_shape=[jax.ShapeDtypeStruct((H, BPD, BLOCK, HD...  206 us
    unnamed x20, local copies, waits for them, and re-layouts  9.95 us

profile of v5, /device:TPU:16, one launch (start us, length us, event | category | flops | bytes accessed | tf_op | source)
XLA Modules:
  0.0 219.1 jit_solution(8526670038627195126)
XLA Ops:
  0.6 0.0 copy-start.6
  0.7 0.7 copy-done.6
  1.3 0.1 reshape.46
  1.5 0.2 copy.22
  1.7 0.1 reshape.47
  1.8 0.7 copy.23.links
  2.4 0.0 copy-start
  2.4 2.0 copy.20
  4.4 0.0 copy-done
  4.4 0.0 copy-start.4
  4.4 0.0 copy-start.5
  4.4 0.9 copy.21
  5.3 0.3 copy-done.4
  5.6 0.2 copy-done.5
  5.8 0.2 copy_bitcast_fusion
  6.0 1.1 pad_maximum_fusion
  7.1 206.1 %shard_map.84 = (bf16[4,8,64,128]{3,2,1,0:T(8,128)(2,1)}, bf16[4,8,64,128]{3,2,1,0:T(8,128)(2,1)}, bf16[4,8,64,128]{3,2,1,0:T(8,128)(2,1)}, bf16[4,8,64,128]{3,2,1,0:T(8,128)(2,1)}) custom-call(bf16[8,8,64,128]{3,2,1,0:T(8,128)(2,1)} %bitcast.36, bf16[4,8,64,128]{3,2,1,0:T(8,128)(2,1)} %bitcast.37, bf16[4,8,64,128]{3,2,1,0:T(8,128)(2,1)} %bitcast.38, ...), custom_call_target="tpu_custom_call" | custom-call | flops 1610612736 | bytes 4194304 | tf_op jit(solution)/shard_map/pallas_call | solution.py:753
  213.2 0.0 copy-start.3
  213.2 2.3 %copy.24 = bf16[512,4,128]{2,1,0:T(4,128)(2,1)} copy(bf16[512,4,128]{2,0,1:T(8,128)(2,1)} %bitcast.42) | data formatting | bytes 1048576
  215.5 0.0 copy-done.3
  215.5 0.0 copy-start.2
  215.5 1.2 copy.25
  216.7 0.0 copy-done.2
  216.7 0.0 copy-start.1
  216.7 1.2 copy.26
  217.9 0.0 copy-done.1
  217.9 1.2 copy.27
  (1 shorter events, 0.0 us)
Async XLA Ops:
  0.6 0.7 copy-start.6
  2.4 2.0 copy-start
  4.4 1.2 copy-start.4
  4.4 1.4 copy-start.5
  213.2 2.3 %copy-start.3 = (bf16[4,8,64,128]{3,2,1,0:T(8,128)(2,1)S(1)}, bf16[4,8,64,128]{3,2,1,0:T(8,128)(2,1)}, u32[]{:S(2)}) copy-start(bf16[4,8,64,128]{3,2,1,0:T(8,128)(2,1)} %get-tuple-element.9) | copy-start | bytes 1572868
  215.5 1.2 copy-start.2
  216.7 1.2 copy-start.1

commit v6 on v5

--- a/solution.py
+++ b/solution.py
@@ -30,8 +30,6 @@
 T_RELAY = RECEIVED
 T_GIVER = T_RELAY + 2 * RELAY
 T_PLACE = T_GIVER + RECEIVED
-T_RIGHT = T_PLACE + REFS
-T_LEFT = T_RIGHT + 1
 T_WIDTH = 256
 PIECES = 2
 DEEP = 8
@@ -57,17 +55,16 @@
         return array[:, e : e + 1]
 
     rank = jnp.zeros_like(named)
-    n_r, n_o, n_l = (jnp.zeros((NX * H, 1), jnp.int32) for _ in range(3))
+    n_r, n_o = (jnp.zeros((NX * H, 1), jnp.int32) for _ in range(2))
     for e in range(REFS):
         way = entry(away, e)
         rank += jnp.where((away == way) & (lane > e), 1, 0)
         n_r += jnp.where(way == 1, 1, 0)
         n_o += jnp.where(way == 2, 1, 0)
-        n_l += jnp.where(way == 3, 1, 0)
     by_right = jnp.minimum(n_o, jnp.minimum(RELAY, MAIN - n_r))
     right_way = rank < by_right
     relay_rank = jnp.where(right_way, rank, rank - by_right)
-    opposite = jnp.where(right_way, FROM_R + n_r + rank, FROM_L + n_l + relay_rank)
+    opposite = jnp.where(right_way, FROM_R, FROM_L) + MAIN - 1 - relay_rank
     place = jnp.where(
         away == 0,
         OWN + rank,
@@ -78,7 +75,7 @@
         away == 2, T_RELAY + relay_rank + jnp.where(right_way, 0, RELAY), -1
     )
     spots = lax.broadcasted_iota(jnp.int32, (NX * H, T_WIDTH), 1)
-    first = jnp.where(spots == T_RIGHT, n_r, jnp.where(spots == T_LEFT, n_l, 0))
+    first = jnp.zeros_like(spots)
     for e in range(REFS):
         here = entry(place, e)
         at = jnp.where(
@@ -104,7 +101,7 @@
         jnp.where(
             spots < T_GIVER,
             TARGETS - 1,
-            jnp.where(spots < T_PLACE, REFS - 1, jnp.where(spots < T_RIGHT, RECEIVED - 1, REFS)),
+            jnp.where(spots < T_PLACE, REFS - 1, RECEIVED - 1),
         ),
     )
     first = jnp.clip(first, 0, most)
@@ -142,38 +139,37 @@
 ORDER = (
     ("GS", 0), ("G", 0, 2, 0), ("G", 0, 2, 1), ("G", 0, 3, 0), ("G", 0, 3, 1), ("GS", 1),
     ("G", 0, 4, 0), ("G", 0, 4, 1), ("G", 1, 2, 0), ("G", 1, 2, 1), ("GE", 0), ("SR", 0),
-    ("G", 1, 3, 0), ("G", 1, 3, 1), ("GS", 2), ("SM", 0), ("G", 1, 4, 0), ("G", 1, 4, 1),
-    ("G", 2, 2, 0), ("GE", 1), ("G", 2, 2, 1), ("SR", 1), ("G", 2, 3, 0), ("G", 2, 3, 1),
-    ("GS", 3), ("G", 2, 4, 0), ("SM", 1), ("G", 2, 4, 1), ("G", 3, 2, 0), ("GE", 2),
-    ("G", 3, 2, 1), ("SR", 2), ("G", 3, 3, 0), ("C", 0, 0), ("SM", 2), ("G", 3, 3, 1), ("GS", 4),
-    ("C", 0, 1), ("G", 3, 4, 0), ("G", 3, 4, 1), ("ST", 0), ("G", 4, 2, 0), ("G", 4, 2, 1),
-    ("ST", 1), ("G", 4, 3, 0), ("GE", 3), ("G", 4, 3, 1), ("GS", 5), ("SR", 3), ("G", 4, 4, 0),
-    ("RT", 0), ("G", 4, 4, 1), ("G", 5, 2, 0), ("G", 5, 2, 1), ("G", 5, 3, 0), ("GE", 4),
-    ("G", 5, 3, 1), ("GS", 6), ("RT", 1), ("G", 5, 4, 0), ("SM", 3), ("G", 5, 4, 1),
-    ("G", 6, 2, 0), ("SR", 4), ("L", 0), ("G", 6, 2, 1), ("R", 0, 2), ("GE", 5), ("SR", 5),
-    ("R", 0, 3), ("G", 6, 3, 0), ("R", 0, 1), ("SM", 4), ("L", 1), ("R", 1, 2), ("R", 1, 1),
-    ("G", 6, 3, 1), ("SS", 0), ("GS", 7), ("C", 1, 0), ("SM", 5), ("G", 6, 4, 0), ("G", 7, 2, 0),
-    ("C", 1, 1), ("SS", 1), ("S", 0, 2, 0), ("ST", 2), ("R", 1, 5), ("G", 6, 4, 1), ("R", 1, 3),
-    ("R", 0, 4), ("S", 1, 2, 0), ("ST", 3), ("C", 2, 0), ("G", 7, 2, 1), ("S", 0, 2, 1), ("RT", 2),
-    ("GE", 6), ("S", 1, 2, 1), ("G", 7, 3, 0), ("C", 2, 1), ("S", 0, 3, 0), ("R", 1, 4),
-    ("G", 7, 3, 1), ("RT", 3), ("ST", 5), ("L", 2), ("S", 1, 3, 0), ("R", 2, 2), ("S", 1, 3, 1),
-    ("G", 7, 4, 0), ("L", 3), ("G", 7, 4, 1), ("S", 1, 4, 0), ("R", 3, 1), ("S", 1, 4, 1),
-    ("R", 3, 5), ("S", 0, 3, 1), ("SS", 3), ("SR", 6), ("S", 0, 4, 0), ("R", 3, 3), ("R", 2, 1),
-    ("R", 3, 2), ("GE", 7), ("R", 2, 3), ("SR", 7), ("S", 0, 4, 1), ("F", 1), ("SM", 6),
-    ("S", 3, 2, 0), ("R", 2, 4), ("SS", 2), ("R", 3, 4), ("S", 3, 2, 1), ("R", 0, 5),
-    ("S", 3, 3, 0), ("SM", 7), ("ST", 4), ("F", 0), ("S", 2, 2, 0), ("RT", 5), ("S", 2, 2, 1),
-    ("S", 2, 3, 0), ("S", 3, 3, 1), ("R", 2, 5), ("S", 2, 3, 1), ("S", 2, 4, 0), ("C", 3, 0),
-    ("S", 3, 4, 0), ("S", 2, 4, 1), ("S", 3, 4, 1), ("RT", 4), ("C", 3, 1), ("L", 5), ("R", 5, 1),
-    ("SS", 5), ("ST", 6), ("R", 5, 2), ("ST", 7), ("L", 4), ("R", 4, 1), ("SS", 4), ("R", 4, 2),
-    ("F", 3), ("S", 5, 2, 0), ("R", 4, 3), ("S", 5, 2, 1), ("R", 4, 4), ("F", 2), ("S", 4, 2, 0),
-    ("R", 5, 5), ("S", 4, 2, 1), ("R", 5, 3), ("S", 5, 3, 0), ("S", 4, 3, 0), ("R", 5, 4),
-    ("R", 4, 5), ("S", 4, 3, 1), ("S", 5, 3, 1), ("RT", 6), ("RT", 7), ("S", 4, 4, 0),
-    ("S", 5, 4, 0), ("L", 6), ("S", 4, 4, 1), ("R", 6, 2), ("R", 6, 1), ("SS", 6), ("S", 5, 4, 1),
-    ("L", 7), ("R", 7, 3), ("R", 7, 1), ("R", 7, 2), ("SS", 7), ("F", 4), ("S", 6, 2, 0),
-    ("S", 6, 2, 1), ("F", 5), ("R", 6, 3), ("S", 7, 2, 0), ("R", 6, 5), ("S", 7, 2, 1),
-    ("R", 6, 4), ("S", 6, 3, 0), ("R", 7, 4), ("S", 7, 3, 0), ("S", 7, 3, 1), ("S", 6, 3, 1),
-    ("R", 7, 5), ("S", 7, 4, 0), ("S", 6, 4, 0), ("S", 6, 4, 1), ("S", 7, 4, 1), ("F", 6),
-    ("F", 7),
+    ("G", 1, 3, 0), ("G", 1, 3, 1), ("GS", 2), ("G", 1, 4, 0), ("SM", 0), ("G", 1, 4, 1),
+    ("G", 2, 2, 0), ("G", 2, 2, 1), ("GE", 1), ("SR", 1), ("G", 2, 3, 0), ("G", 2, 3, 1),
+    ("G", 2, 4, 0), ("SM", 1), ("G", 2, 4, 1), ("GS", 3), ("GE", 2), ("SR", 2), ("G", 3, 2, 0),
+    ("C", 0, 0), ("G", 3, 2, 1), ("SM", 2), ("C", 0, 1), ("ST", 1), ("G", 3, 3, 0), ("ST", 0),
+    ("G", 3, 3, 1), ("GS", 4), ("G", 3, 4, 0), ("G", 3, 4, 1), ("G", 4, 2, 0), ("G", 4, 2, 1),
+    ("G", 4, 3, 0), ("RT", 1), ("RT", 0), ("GE", 3), ("G", 4, 3, 1), ("GS", 5), ("SR", 3),
+    ("G", 4, 4, 0), ("G", 5, 2, 0), ("L", 1), ("G", 5, 2, 1), ("G", 4, 4, 1), ("L", 0),
+    ("R", 1, 2), ("G", 5, 3, 0), ("SM", 3), ("R", 1, 5), ("G", 5, 3, 1), ("R", 0, 1), ("GS", 6),
+    ("GE", 4), ("R", 1, 1), ("R", 0, 3), ("R", 1, 3), ("G", 5, 4, 0), ("SR", 4), ("G", 5, 4, 1),
+    ("G", 6, 2, 0), ("SS", 1), ("GE", 5), ("G", 6, 2, 1), ("SR", 5), ("R", 0, 2), ("SS", 0),
+    ("R", 0, 5), ("G", 6, 3, 0), ("C", 1, 0), ("G", 6, 3, 1), ("SM", 4), ("S", 1, 2, 0), ("GS", 7),
+    ("SM", 5), ("C", 1, 1), ("S", 1, 2, 1), ("ST", 2), ("S", 1, 3, 0), ("G", 6, 4, 0),
+    ("G", 7, 2, 0), ("S", 0, 2, 0), ("R", 0, 4), ("G", 7, 2, 1), ("S", 0, 2, 1), ("R", 1, 4),
+    ("S", 1, 3, 1), ("RT", 2), ("G", 6, 4, 1), ("ST", 3), ("C", 2, 0), ("G", 7, 3, 0),
+    ("G", 7, 3, 1), ("C", 2, 1), ("S", 1, 4, 0), ("S", 0, 3, 0), ("L", 2), ("S", 0, 3, 1),
+    ("RT", 3), ("S", 1, 4, 1), ("ST", 5), ("S", 0, 4, 0), ("L", 3), ("R", 3, 1), ("R", 3, 5),
+    ("SS", 3), ("G", 7, 4, 0), ("F", 1), ("R", 2, 4), ("R", 2, 2), ("RT", 5), ("S", 0, 4, 1),
+    ("R", 3, 2), ("R", 2, 1), ("S", 3, 2, 0), ("S", 3, 2, 1), ("R", 3, 4), ("R", 3, 3), ("GE", 6),
+    ("G", 7, 4, 1), ("R", 2, 3), ("SR", 6), ("S", 3, 3, 0), ("S", 3, 3, 1), ("SS", 2), ("L", 5),
+    ("SM", 6), ("GE", 7), ("S", 3, 4, 0), ("R", 5, 2), ("SR", 7), ("R", 5, 5), ("R", 2, 5),
+    ("S", 3, 4, 1), ("R", 5, 1), ("F", 0), ("SS", 5), ("S", 2, 2, 0), ("S", 2, 2, 1), ("F", 3),
+    ("S", 5, 2, 0), ("SM", 7), ("S", 2, 3, 0), ("R", 5, 4), ("ST", 4), ("R", 5, 3), ("S", 5, 2, 1),
+    ("S", 2, 3, 1), ("S", 5, 3, 0), ("S", 2, 4, 0), ("C", 3, 0), ("S", 5, 3, 1), ("RT", 4),
+    ("S", 2, 4, 1), ("C", 3, 1), ("ST", 7), ("S", 5, 4, 0), ("L", 4), ("R", 4, 1), ("SS", 4),
+    ("F", 2), ("R", 4, 2), ("S", 5, 4, 1), ("S", 4, 2, 0), ("R", 4, 4), ("S", 4, 2, 1), ("RT", 7),
+    ("R", 4, 3), ("S", 4, 3, 0), ("ST", 6), ("S", 4, 3, 1), ("R", 4, 5), ("L", 7), ("R", 7, 1),
+    ("SS", 7), ("F", 5), ("S", 4, 4, 0), ("R", 7, 2), ("R", 7, 3), ("RT", 6), ("S", 7, 2, 0),
+    ("S", 4, 4, 1), ("R", 7, 4), ("S", 7, 2, 1), ("S", 7, 3, 0), ("L", 6), ("R", 6, 1), ("SS", 6),
+    ("S", 7, 3, 1), ("R", 6, 3), ("S", 7, 4, 0), ("R", 6, 2), ("R", 6, 5), ("F", 4),
+    ("S", 6, 2, 0), ("S", 6, 2, 1), ("R", 6, 4), ("S", 7, 4, 1), ("S", 6, 3, 0), ("S", 6, 3, 1),
+    ("S", 6, 4, 0), ("R", 7, 5), ("S", 6, 4, 1), ("F", 7), ("F", 6),
 )
 
 
@@ -319,12 +315,15 @@
             (x_r, x_l)[side], relay_out[u].at[side], relay_in[u].at[1 - side], x_sem.at[0, u, side]
         )
 
-    def merged_copy(u, side):
+    def part_of(start, part):
+        return pl.ds(start + part * RELAY, RELAY)
+
+    def merged_copy(u, side, part):
         return to(
             (x_r, x_l)[side],
-            merged_out[u].at[side],
-            received[u].at[pl.ds((FROM_L, FROM_R)[side], MAIN)],
-            x_sem.at[1, u, side],
+            merged_out[u].at[side, part_of(0, part)],
+            received[u].at[part_of((FROM_L, FROM_R)[side], part)],
+            x_sem.at[(4, 1)[part], u, side],
         )
 
     def anchor_copy(u, side):
@@ -365,6 +364,15 @@
         for side in (0, 1):
             relay_copy(u, side).start()
 
+        @pl.loop(0, RELAY)
+        def _(k):
+            for side, plane, first in ((0, p_r, FROM_L), (1, p_l, FROM_R)):
+                code = slot_t[plane * H + h, first + k]
+                merged_out[u][side, k] = table[u][jnp.minimum(code, TARGETS - 1)]
+
+        for side in (0, 1):
+            merged_copy(u, side, 0).start()
+
         @pl.loop(0, MAIN)
         def _(k):
             received[u][OWN + k] = table[u][slot_t[x * H + h, OWN + k]]
@@ -374,16 +382,18 @@
         for side in (0, 1):
             relay_copy(u, side).wait_recv()
 
-        @pl.loop(0, MAIN)
+        @pl.loop(0, RELAY)
         def _(k):
+            spot = MAIN - 1 - k
             for side, plane, first, back in ((0, p_r, FROM_L, 1), (1, p_l, FROM_R, 0)):
-                code = slot_t[plane * H + h, first + k]
+                code = slot_t[plane * H + h, first + spot]
                 direct = table[u][jnp.minimum(code, TARGETS - 1)]
-                passed = relay_in[u][back, jnp.maximum(code - TARGETS, 0)]
-                merged_out[u][side, k] = jnp.where(code < TARGETS, direct, passed)
+                merged_out[u][side, spot] = jnp.where(
+                    code < TARGETS, direct, relay_in[u][back, k]
+                )
 
         for side in (0, 1):
-            merged_copy(u, side).start()
+            merged_copy(u, side, 1).start()
         anchor_arrived(u)
 
         @pl.when(inner)
@@ -397,7 +407,8 @@
         for p in (0, 1):
             u = 2 * h + p
             for side in (0, 1):
-                merged_copy(u, side).wait_recv()
+                for part in (0, 1):
+                    merged_copy(u, side, part).wait_recv()
 
             @pl.when(inner)
             def _():
@@ -470,12 +481,12 @@
                 for r in range(R):
                     terms[p, i * R + r] = part[(5 + r) * BLOCK : (6 + r) * BLOCK].astype(BF16)
 
-    def terms_copy(u, side):
+    def terms_copy(u, side, part):
         return to(
             (x_r, x_l)[side],
-            merged_out[u].at[side],
-            terms_in[u].at[pl.ds((FROM_L, FROM_R)[side], MAIN)],
-            x_sem.at[2, u, side],
+            merged_out[u].at[side, part_of(0, part)],
+            terms_in[u].at[part_of((FROM_L, FROM_R)[side], part)],
+            x_sem.at[(5, 2)[part], u, side],
         )
 
     def terms_relay_copy(u, side):
@@ -508,17 +519,22 @@
 
     def send_terms(u):
         h, p = u // 2, u % 2
-        for side in (0, 1):
-            merged_copy(u, side).wait_send()
+        for part in (1, 0):
+            for side in (0, 1):
+                merged_copy(u, side, part).wait_send()
+
+            @pl.loop(part * RELAY, (part + 1) * RELAY)
+            def _(k):
+                merged_out[u][0, k] = terms[p, slot_t[x * H + h, T_GIVER + FROM_R + k]]
+                merged_out[u][1, k] = terms[p, slot_t[x * H + h, T_GIVER + FROM_L + k]]
+
+            for side in (0, 1):
+                terms_copy(u, side, part).start()
 
         @pl.loop(0, MAIN)
         def _(k):
-            merged_out[u][0, k] = terms[p, slot_t[x * H + h, T_GIVER + FROM_R + k]]
-            merged_out[u][1, k] = terms[p, slot_t[x * H + h, T_GIVER + FROM_L + k]]
             terms_in[u][B_OWN + k] = terms[p, slot_t[x * H + h, T_GIVER + OWN + k]]
 
-        for side in (0, 1):
-            terms_copy(u, side).start()
         terms_in[u][B_ZERO] = jnp.zeros((BLOCK, HD), BF16)
 
         @pl.when(inner)
@@ -532,17 +548,14 @@
             edge_part_copy(u).start()
 
     def relay_terms(u):
-        h = u // 2
         for side in (0, 1):
             relay_copy(u, side).wait_send()
-            terms_copy(u, side).wait_recv()
+            terms_copy(u, side, 1).wait_recv()
 
         @pl.loop(0, RELAY)
         def _(k):
-            from_left = slot_t[p_l * H + h, T_RIGHT] + k
-            from_right = slot_t[p_r * H + h, T_LEFT] + k
-            relay_out[u][0, k] = terms_in[u][FROM_L + jnp.minimum(from_left, MAIN - 1)]
-            relay_out[u][1, k] = terms_in[u][FROM_R + jnp.minimum(from_right, MAIN - 1)]
+            relay_out[u][0, k] = terms_in[u][FROM_L + MAIN - 1 - k]
+            relay_out[u][1, k] = terms_in[u][FROM_R + MAIN - 1 - k]
 
         for side in (0, 1):
             terms_relay_copy(u, side).start()
@@ -575,6 +588,7 @@
                 part_second(u, side).wait_recv()
 
         for side in (0, 1):
+            terms_copy(u, side, 0).wait_recv()
             terms_relay_copy(u, side).wait_recv()
 
         @pl.loop(0, RELAY)
@@ -679,7 +693,8 @@
     def drain(u):
         all_sent(u, rs_sent)
         for side in (0, 1):
-            terms_copy(u, side).wait_send()
+            for part in (0, 1):
+                terms_copy(u, side, part).wait_send()
             terms_relay_copy(u, side).wait_send()
 
         @pl.when(inner)
@@ -781,7 +796,7 @@
             dma((2, 4, 2, 2)),
             dma((UNITS,)),
             dma((2, 4, 2, 2)),
-            dma((4, UNITS, 2, 2)),
+            dma((6, UNITS, 2, 2)),
             dma((UNITS, 3, 2)),
             dma((UNITS, 3, 2)),
             dma((UNITS + 1, 2)),

time: 219 us -> 215 us (0.982)
  Pallas kernels: 206 us -> 202 us
    pallas_call x1, Pallas kernels: 206 us -> 202 us  [local(): pl.pallas_call(kernel, out_shape=[jax.ShapeDtypeStruct((H, BPD, BLOCK, HD...]
where the time goes in v6:
time: 215 us
  Pallas kernels  202 us (94%)
  local copies, waits for them, and re-layouts  11.3 us (5%)
    pallas_call x1, Pallas kernels, local(): pl.pallas_call(kernel, out_shape=[jax.ShapeDtypeStruct((H, BPD, BLOCK, HD...  202 us
    unnamed x20, local copies, waits for them, and re-layouts  9.95 us

profile of v6, /device:TPU:16, one launch (start us, length us, event | category | flops | bytes accessed | tf_op | source)
XLA Modules:
  0.0 214.6 jit_solution(2193406956258381769)
XLA Ops:
  0.6 0.0 copy-start.6
  0.7 0.7 copy-done.6
  1.3 0.1 reshape.46
  1.5 0.2 copy.22
  1.7 0.1 reshape.47
  1.8 0.7 copy.23.links
  2.4 0.0 copy-start
  2.4 2.0 copy.20
  4.4 0.0 copy-done
  4.4 0.0 copy-start.4
  4.4 0.0 copy-start.5
  4.4 0.9 copy.21
  5.3 0.3 copy-done.4
  5.6 0.2 copy-done.5
  5.8 0.2 copy_bitcast_fusion
  6.0 1.1 pad_maximum_fusion
  7.1 201.6 %shard_map.84 = (bf16[4,8,64,128]{3,2,1,0:T(8,128)(2,1)}, bf16[4,8,64,128]{3,2,1,0:T(8,128)(2,1)}, bf16[4,8,64,128]{3,2,1,0:T(8,128)(2,1)}, bf16[4,8,64,128]{3,2,1,0:T(8,128)(2,1)}) custom-call(bf16[8,8,64,128]{3,2,1,0:T(8,128)(2,1)} %bitcast.36, bf16[4,8,64,128]{3,2,1,0:T(8,128)(2,1)} %bitcast.37, bf16[4,8,64,128]{3,2,1,0:T(8,128)(2,1)} %bitcast.38, ...), custom_call_target="tpu_custom_call" | custom-call | flops 1610612736 | bytes 4194304 | tf_op jit(solution)/shard_map/pallas_call | solution.py:768
  208.7 0.0 copy-start.3
  208.7 2.3 %copy.24 = bf16[512,4,128]{2,1,0:T(4,128)(2,1)} copy(bf16[512,4,128]{2,0,1:T(8,128)(2,1)} %bitcast.42) | data formatting | bytes 1048576
  211.0 0.0 copy-done.3
  211.0 0.0 copy-start.2
  211.0 1.2 copy.25
  212.2 0.0 copy-done.2
  212.2 0.0 copy-start.1
  212.2 1.2 copy.26
  213.4 0.0 copy-done.1
  213.4 1.2 copy.27
  (1 shorter events, 0.0 us)
Async XLA Ops:
  0.6 0.7 copy-start.6
  2.4 2.0 copy-start
  4.4 1.2 copy-start.4
  4.4 1.4 copy-start.5
  208.7 2.3 %copy-start.3 = (bf16[4,8,64,128]{3,2,1,0:T(8,128)(2,1)S(1)}, bf16[4,8,64,128]{3,2,1,0:T(8,128)(2,1)}, u32[]{:S(2)}) copy-start(bf16[4,8,64,128]{3,2,1,0:T(8,128)(2,1)} %get-tuple-element.9) | copy-start | bytes 1572868
  211.0 1.2 copy-start.2
  212.2 1.2 copy-start.1

commit v7 on v6

--- a/solution.py
+++ b/solution.py
@@ -139,37 +139,38 @@
 ORDER = (
     ("GS", 0), ("G", 0, 2, 0), ("G", 0, 2, 1), ("G", 0, 3, 0), ("G", 0, 3, 1), ("GS", 1),
     ("G", 0, 4, 0), ("G", 0, 4, 1), ("G", 1, 2, 0), ("G", 1, 2, 1), ("GE", 0), ("SR", 0),
-    ("G", 1, 3, 0), ("G", 1, 3, 1), ("GS", 2), ("G", 1, 4, 0), ("SM", 0), ("G", 1, 4, 1),
+    ("G", 1, 3, 0), ("G", 1, 3, 1), ("GS", 2), ("SM", 0), ("G", 1, 4, 0), ("G", 1, 4, 1),
     ("G", 2, 2, 0), ("G", 2, 2, 1), ("GE", 1), ("SR", 1), ("G", 2, 3, 0), ("G", 2, 3, 1),
     ("G", 2, 4, 0), ("SM", 1), ("G", 2, 4, 1), ("GS", 3), ("GE", 2), ("SR", 2), ("G", 3, 2, 0),
-    ("C", 0, 0), ("G", 3, 2, 1), ("SM", 2), ("C", 0, 1), ("ST", 1), ("G", 3, 3, 0), ("ST", 0),
-    ("G", 3, 3, 1), ("GS", 4), ("G", 3, 4, 0), ("G", 3, 4, 1), ("G", 4, 2, 0), ("G", 4, 2, 1),
-    ("G", 4, 3, 0), ("RT", 1), ("RT", 0), ("GE", 3), ("G", 4, 3, 1), ("GS", 5), ("SR", 3),
-    ("G", 4, 4, 0), ("G", 5, 2, 0), ("L", 1), ("G", 5, 2, 1), ("G", 4, 4, 1), ("L", 0),
-    ("R", 1, 2), ("G", 5, 3, 0), ("SM", 3), ("R", 1, 5), ("G", 5, 3, 1), ("R", 0, 1), ("GS", 6),
-    ("GE", 4), ("R", 1, 1), ("R", 0, 3), ("R", 1, 3), ("G", 5, 4, 0), ("SR", 4), ("G", 5, 4, 1),
-    ("G", 6, 2, 0), ("SS", 1), ("GE", 5), ("G", 6, 2, 1), ("SR", 5), ("R", 0, 2), ("SS", 0),
-    ("R", 0, 5), ("G", 6, 3, 0), ("C", 1, 0), ("G", 6, 3, 1), ("SM", 4), ("S", 1, 2, 0), ("GS", 7),
-    ("SM", 5), ("C", 1, 1), ("S", 1, 2, 1), ("ST", 2), ("S", 1, 3, 0), ("G", 6, 4, 0),
-    ("G", 7, 2, 0), ("S", 0, 2, 0), ("R", 0, 4), ("G", 7, 2, 1), ("S", 0, 2, 1), ("R", 1, 4),
-    ("S", 1, 3, 1), ("RT", 2), ("G", 6, 4, 1), ("ST", 3), ("C", 2, 0), ("G", 7, 3, 0),
-    ("G", 7, 3, 1), ("C", 2, 1), ("S", 1, 4, 0), ("S", 0, 3, 0), ("L", 2), ("S", 0, 3, 1),
-    ("RT", 3), ("S", 1, 4, 1), ("ST", 5), ("S", 0, 4, 0), ("L", 3), ("R", 3, 1), ("R", 3, 5),
-    ("SS", 3), ("G", 7, 4, 0), ("F", 1), ("R", 2, 4), ("R", 2, 2), ("RT", 5), ("S", 0, 4, 1),
-    ("R", 3, 2), ("R", 2, 1), ("S", 3, 2, 0), ("S", 3, 2, 1), ("R", 3, 4), ("R", 3, 3), ("GE", 6),
-    ("G", 7, 4, 1), ("R", 2, 3), ("SR", 6), ("S", 3, 3, 0), ("S", 3, 3, 1), ("SS", 2), ("L", 5),
-    ("SM", 6), ("GE", 7), ("S", 3, 4, 0), ("R", 5, 2), ("SR", 7), ("R", 5, 5), ("R", 2, 5),
-    ("S", 3, 4, 1), ("R", 5, 1), ("F", 0), ("SS", 5), ("S", 2, 2, 0), ("S", 2, 2, 1), ("F", 3),
-    ("S", 5, 2, 0), ("SM", 7), ("S", 2, 3, 0), ("R", 5, 4), ("ST", 4), ("R", 5, 3), ("S", 5, 2, 1),
-    ("S", 2, 3, 1), ("S", 5, 3, 0), ("S", 2, 4, 0), ("C", 3, 0), ("S", 5, 3, 1), ("RT", 4),
-    ("S", 2, 4, 1), ("C", 3, 1), ("ST", 7), ("S", 5, 4, 0), ("L", 4), ("R", 4, 1), ("SS", 4),
-    ("F", 2), ("R", 4, 2), ("S", 5, 4, 1), ("S", 4, 2, 0), ("R", 4, 4), ("S", 4, 2, 1), ("RT", 7),
-    ("R", 4, 3), ("S", 4, 3, 0), ("ST", 6), ("S", 4, 3, 1), ("R", 4, 5), ("L", 7), ("R", 7, 1),
-    ("SS", 7), ("F", 5), ("S", 4, 4, 0), ("R", 7, 2), ("R", 7, 3), ("RT", 6), ("S", 7, 2, 0),
-    ("S", 4, 4, 1), ("R", 7, 4), ("S", 7, 2, 1), ("S", 7, 3, 0), ("L", 6), ("R", 6, 1), ("SS", 6),
-    ("S", 7, 3, 1), ("R", 6, 3), ("S", 7, 4, 0), ("R", 6, 2), ("R", 6, 5), ("F", 4),
-    ("S", 6, 2, 0), ("S", 6, 2, 1), ("R", 6, 4), ("S", 7, 4, 1), ("S", 6, 3, 0), ("S", 6, 3, 1),
-    ("S", 6, 4, 0), ("R", 7, 5), ("S", 6, 4, 1), ("F", 7), ("F", 6),
+    ("C", 0, 0), ("G", 3, 2, 1), ("G", 3, 3, 0), ("SM", 2), ("C", 0, 1), ("ST", 0), ("G", 3, 3, 1),
+    ("GS", 4), ("G", 3, 4, 0), ("ST", 1), ("G", 4, 2, 0), ("G", 4, 2, 1), ("G", 3, 4, 1),
+    ("G", 4, 3, 0), ("G", 4, 3, 1), ("GS", 5), ("GE", 3), ("SR", 3), ("G", 5, 2, 0),
+    ("G", 5, 2, 1), ("SM", 3), ("G", 4, 4, 0), ("RT", 1), ("G", 4, 4, 1), ("G", 5, 3, 0),
+    ("G", 5, 3, 1), ("GS", 6), ("RT", 0), ("GE", 4), ("SR", 4), ("C", 1, 0), ("L", 1),
+    ("G", 5, 4, 0), ("R", 1, 1), ("G", 6, 2, 0), ("G", 5, 4, 1), ("SS", 1), ("R", 1, 5),
+    ("R", 1, 2), ("C", 1, 1), ("L", 0), ("G", 6, 2, 1), ("ST", 3), ("GE", 5), ("R", 0, 1),
+    ("ST", 2), ("SS", 0), ("G", 6, 3, 0), ("G", 6, 3, 1), ("S", 1, 2, 0), ("SR", 5),
+    ("G", 6, 4, 0), ("GS", 7), ("R", 0, 2), ("S", 1, 2, 1), ("G", 7, 2, 0), ("G", 6, 4, 1),
+    ("S", 0, 2, 0), ("G", 7, 2, 1), ("G", 7, 3, 0), ("S", 0, 2, 1), ("RT", 2), ("R", 0, 5),
+    ("R", 0, 3), ("G", 7, 3, 1), ("S", 0, 3, 0), ("R", 0, 4), ("RT", 3), ("R", 1, 3),
+    ("S", 0, 3, 1), ("GE", 6), ("S", 1, 3, 0), ("SM", 5), ("SM", 4), ("S", 1, 3, 1), ("L", 2),
+    ("L", 3), ("R", 3, 1), ("G", 7, 4, 0), ("R", 3, 2), ("R", 1, 4), ("SR", 6), ("G", 7, 4, 1),
+    ("R", 2, 3), ("S", 0, 4, 0), ("R", 2, 2), ("S", 0, 4, 1), ("R", 2, 5), ("R", 2, 1),
+    ("S", 1, 4, 0), ("SS", 2), ("GE", 7), ("SR", 7), ("S", 1, 4, 1), ("R", 3, 3), ("C", 2, 0),
+    ("SS", 3), ("F", 0), ("S", 2, 2, 0), ("S", 2, 2, 1), ("C", 2, 1), ("ST", 4), ("R", 3, 4),
+    ("F", 1), ("S", 2, 3, 0), ("S", 3, 2, 0), ("R", 2, 4), ("S", 3, 2, 1), ("S", 2, 3, 1),
+    ("S", 3, 3, 0), ("RT", 4), ("S", 3, 3, 1), ("S", 2, 4, 0), ("SM", 6), ("S", 2, 4, 1),
+    ("SM", 7), ("L", 4), ("R", 4, 1), ("SS", 4), ("R", 4, 2), ("S", 3, 4, 0), ("S", 3, 4, 1),
+    ("F", 2), ("ST", 5), ("R", 4, 3), ("S", 4, 2, 0), ("S", 4, 2, 1), ("C", 3, 0), ("RT", 5),
+    ("S", 4, 3, 0), ("C", 3, 1), ("ST", 6), ("S", 4, 3, 1), ("L", 5), ("R", 5, 1), ("SS", 5),
+    ("R", 4, 4), ("R", 3, 5), ("S", 4, 4, 0), ("S", 4, 4, 1), ("F", 3), ("R", 5, 2), ("RT", 6),
+    ("R", 4, 5), ("S", 5, 2, 0), ("S", 5, 2, 1), ("R", 5, 3), ("ST", 7), ("S", 5, 3, 0),
+    ("S", 5, 3, 1), ("F", 4), ("L", 6), ("R", 6, 5), ("R", 5, 4), ("R", 6, 1), ("SS", 6),
+    ("S", 5, 4, 0), ("RT", 7), ("R", 6, 3), ("R", 6, 2), ("S", 5, 4, 1), ("S", 6, 2, 0),
+    ("S", 6, 2, 1), ("L", 7), ("R", 7, 1), ("SS", 7), ("R", 7, 3), ("S", 6, 3, 0), ("R", 6, 4),
+    ("S", 6, 3, 1), ("R", 7, 2), ("R", 5, 5), ("F", 5), ("S", 7, 2, 0), ("S", 7, 2, 1),
+    ("S", 6, 4, 0), ("S", 7, 3, 0), ("S", 7, 3, 1), ("R", 7, 4), ("S", 6, 4, 1), ("S", 7, 4, 0),
+    ("S", 7, 4, 1), ("R", 7, 5), ("F", 6), ("F", 7),
 )
 
 

time: 215 us -> 215 us (level)
  no operation moved by 1% of the time
where the time goes in v7:
time: 215 us
  Pallas kernels  202 us (94%)
  local copies, waits for them, and re-layouts  11.3 us (5%)
    pallas_call x1, Pallas kernels, local(): pl.pallas_call(kernel, out_shape=[jax.ShapeDtypeStruct((H, BPD, BLOCK, HD...  202 us
    unnamed x20, local copies, waits for them, and re-layouts  9.95 us

profile of v7, /device:TPU:16, one launch (start us, length us, event | category | flops | bytes accessed | tf_op | source)
XLA Modules:
  0.0 215.1 jit_solution(3846667650830774171)
XLA Ops:
  0.6 0.0 copy-start.6
  0.7 0.7 copy-done.6
  1.3 0.1 reshape.46
  1.5 0.2 copy.22
  1.7 0.1 reshape.47
  1.8 0.7 copy.23.links
  2.4 0.0 copy-start
  2.4 2.0 copy.20
  4.4 0.0 copy-done
  4.4 0.0 copy-start.4
  4.4 0.0 copy-start.5
  4.4 0.9 copy.21
  5.3 0.3 copy-done.4
  5.6 0.2 copy-done.5
  5.8 0.2 copy_bitcast_fusion
  6.0 1.1 pad_maximum_fusion
  7.1 202.1 %shard_map.84 = (bf16[4,8,64,128]{3,2,1,0:T(8,128)(2,1)}, bf16[4,8,64,128]{3,2,1,0:T(8,128)(2,1)}, bf16[4,8,64,128]{3,2,1,0:T(8,128)(2,1)}, bf16[4,8,64,128]{3,2,1,0:T(8,128)(2,1)}) custom-call(bf16[8,8,64,128]{3,2,1,0:T(8,128)(2,1)} %bitcast.36, bf16[4,8,64,128]{3,2,1,0:T(8,128)(2,1)} %bitcast.37, bf16[4,8,64,128]{3,2,1,0:T(8,128)(2,1)} %bitcast.38, ...), custom_call_target="tpu_custom_call" | custom-call | flops 1610612736 | bytes 4194304 | tf_op jit(solution)/shard_map/pallas_call | solution.py:769
  209.2 0.0 copy-start.3
  209.2 2.3 %copy.24 = bf16[512,4,128]{2,1,0:T(4,128)(2,1)} copy(bf16[512,4,128]{2,0,1:T(8,128)(2,1)} %bitcast.42) | data formatting | bytes 1048576
  211.5 0.0 copy-done.3
  211.5 0.0 copy-start.2
  211.5 1.2 copy.25
  212.7 0.0 copy-done.2
  212.7 0.0 copy-start.1
  212.7 1.2 copy.26
  213.9 0.0 copy-done.1
  213.9 1.2 copy.27
  (1 shorter events, 0.0 us)
Async XLA Ops:
  0.6 0.7 copy-start.6
  2.4 2.0 copy-start
  4.4 1.2 copy-start.4
  4.4 1.4 copy-start.5
  209.2 2.3 %copy-start.3 = (bf16[4,8,64,128]{3,2,1,0:T(8,128)(2,1)S(1)}, bf16[4,8,64,128]{3,2,1,0:T(8,128)(2,1)}, u32[]{:S(2)}) copy-start(bf16[4,8,64,128]{3,2,1,0:T(8,128)(2,1)} %get-tuple-element.9) | copy-start | bytes 1572868
  211.5 1.2 copy-start.2
  212.7 1.2 copy-start.1
